TPU v7x, 32 devices: a whole 2x2x4 slice. The times are simulated.
32 devices in a mesh: seq: 8 (over z, x), mp: 4 (over y, core).
Axes of the slice: x: 2, y: 2, z: 4, core: 2. Of those that a mesh axis runs over, the one named last changes fastest.
Arguments:
- queries: bfloat16 [8192, 1024], P('seq', 'mp'), may hold values from -8 to 8
- byte_keys: bfloat16 [8192, 1024], P('seq', 'mp'), may hold values from -8 to 8
- byte_values: bfloat16 [8192, 1024], P('seq', 'mp'), may hold values from -6 to 6
- w_query: bfloat16 [1024, 1024], P(None, 'mp'), may hold values from -0.1875 to 0.1875
- w_key: bfloat16 [1024, 1024], P(None, 'mp'), may hold values from -0.1875 to 0.1875
- w_value: bfloat16 [1024, 1024], P(None, 'mp'), may hold values from -0.1875 to 0.1875
- w_out: bfloat16 [1024, 1024], P('mp'), may hold values from -0.1875 to 0.1875
- d_output: bfloat16 [8192, 1024], P('seq'), may hold values from -96 to 96
- patch_index: int32 [8192], P('seq'), may hold values from 0 to 2047, as said below
- unpatch: bfloat16 [1024, 4096], P(None, 'mp'), may hold values from -0.09375 to 0.09375
Outputs:
- d_patch: bfloat16 [2048, 4096], P('seq', 'mp')
Inputs may be any that keep to these rules, and one draw needn't show every extreme that they name: patch_index never falls and every one of the 2048 patches covers one or more bytes; patch 0 starts at byte 0, and for every k from 1 to 8 - 1 the first byte of patch k * 256 lies 1 to 128 bytes after byte k * 1024, the latter distance reached.
All inputs are finite; a program needn't handle non-finite values.
Results may differ from a plain program's by a relative error of at most 0.025.
Values may be sent and summed in bfloat16 or wider, within the bound.
A program may use at most 128 MiB of HBM per device.

v0:
```python
import jax
import jax.numpy as jnp
from jax import lax
from jax.sharding import PartitionSpec as P

HS = 64
WINDOW = 512
PATCH_DEV = 256


def passed_along(value, axis, steps):
    count = lax.axis_size(axis)
    leading, last = (max(0, -steps), min(count, count - steps))
    return lax.ppermute(value, axis, [(source, source + steps) for source in range(leading, last)])


def block_grads(query_block, grad_block, key_block, value_block, keep_first):
    block_rows = query_block.shape[0]
    head_count = query_block.shape[1] // HS
    factor = HS ** (-0.5)
    query_heads = query_block.reshape(block_rows, head_count, HS)
    grad_heads = grad_block.reshape(block_rows, head_count, HS)
    key_heads = key_block.reshape(2 * block_rows, head_count, HS)
    value_heads = value_block.reshape(2 * block_rows, head_count, HS)
    scores = (
        jnp.einsum("ihd,jhd->hij", query_heads, key_heads, preferred_element_type=jnp.float32)
        * factor
    )
    query_pos = jnp.arange(block_rows, dtype=jnp.int32)[:, None]
    key_pos = jnp.arange(2 * block_rows, dtype=jnp.int32)[None, :]
    allowed = (
        (key_pos > query_pos)
        & (key_pos <= query_pos + block_rows)
        & ((key_pos >= block_rows) | keep_first)
    )
    scores = jnp.where(allowed[None], scores, -1e30)
    peak = jnp.max(scores, axis=-1, keepdims=True)
    raised = jnp.exp(scores - peak)
    attend = raised / jnp.sum(raised, axis=-1, keepdims=True)
    d_attend = jnp.einsum(
        "ihd,jhd->hij", grad_heads, value_heads, preferred_element_type=jnp.float32
    )
    row_dot = jnp.sum(attend * d_attend, axis=-1, keepdims=True)
    d_scores = (attend * (d_attend - row_dot)).astype(jnp.bfloat16)
    attend_low = attend.astype(jnp.bfloat16)
    d_query = (
        jnp.einsum("hij,jhd->ihd", d_scores, key_heads, preferred_element_type=jnp.float32) * factor
    )
    d_key = (
        jnp.einsum("hij,ihd->jhd", d_scores, query_heads, preferred_element_type=jnp.float32)
        * factor
    )
    d_value = jnp.einsum("hij,ihd->jhd", attend_low, grad_heads, preferred_element_type=jnp.float32)
    return (
        d_query.reshape(block_rows, -1),
        d_key.reshape(2 * block_rows, -1),
        d_value.reshape(2 * block_rows, -1),
    )


def spread(parts, width):
    leading = parts[:, :WINDOW].reshape(-1, width)
    trailing = parts[:, WINDOW:].reshape(-1, width)
    blank_rows = jnp.zeros((WINDOW, width), jnp.float32)
    return jnp.concatenate([leading, blank_rows], 0) + jnp.concatenate([blank_rows, trailing], 0)


def on_device(
    queries, byte_keys, byte_values, w_query, w_key, w_value, w_out, d_output, patch_index, unpatch
):
    byte_count = queries.shape[0]
    width = queries.shape[1]
    shard = lax.axis_index("seq")
    grad_all = jnp.dot(d_output, w_out.T, preferred_element_type=jnp.float32).astype(jnp.bfloat16)
    tail_keys, tail_values = passed_along(
        (byte_keys[byte_count - WINDOW :], byte_values[byte_count - WINDOW :]), "seq", 1
    )
    ext_keys = jnp.concatenate([tail_keys, byte_keys], 0)
    ext_values = jnp.concatenate([tail_values, byte_values], 0)

    def one_block(block_id):
        offset = block_id * WINDOW
        return block_grads(
            lax.dynamic_slice_in_dim(queries, offset, WINDOW, 0),
            lax.dynamic_slice_in_dim(grad_all, offset, WINDOW, 0),
            lax.dynamic_slice_in_dim(ext_keys, offset, 2 * WINDOW, 0),
            lax.dynamic_slice_in_dim(ext_values, offset, 2 * WINDOW, 0),
            (block_id > 0) | (shard > 0),
        )

    d_query, key_parts, value_parts = lax.map(
        one_block, jnp.arange(byte_count // WINDOW, dtype=jnp.int32)
    )
    d_query_low = d_query.reshape(byte_count, width).astype(jnp.bfloat16)
    key_ext = spread(key_parts, width)
    value_ext = spread(value_parts, width)
    own_keys = key_ext[WINDOW:]
    own_values = value_ext[WINDOW:]
    head_rows = byte_count - WINDOW
    cross = PATCH_DEV
    local_slot = patch_index - shard * PATCH_DEV + cross
    slots = PATCH_DEV + cross
    next_keys, next_values = (
        passed_along(key_ext[:WINDOW].astype(jnp.bfloat16), "seq", -1).astype(jnp.float32),
        passed_along(value_ext[:WINDOW].astype(jnp.bfloat16), "seq", -1).astype(jnp.float32),
    )
    full_keys = jnp.concatenate([own_keys[:head_rows], own_keys[head_rows:] + next_keys], 0).astype(
        jnp.bfloat16
    )
    full_values = jnp.concatenate(
        [own_values[:head_rows], own_values[head_rows:] + next_values], 0
    ).astype(jnp.bfloat16)
    byte_grad = (
        jnp.dot(d_query_low, w_query.T, preferred_element_type=jnp.float32)
        + jnp.dot(full_keys, w_key.T, preferred_element_type=jnp.float32)
        + jnp.dot(full_values, w_value.T, preferred_element_type=jnp.float32)
    )
    frame = jax.ops.segment_sum(byte_grad, local_slot, num_segments=slots)
    from_next = passed_along(frame[:cross].astype(jnp.bfloat16), "seq", -1).astype(jnp.float32)
    owned = frame[cross:] + from_next
    patch_low = lax.psum(owned.astype(jnp.bfloat16), "mp")
    return jnp.dot(patch_low, unpatch, preferred_element_type=jnp.float32).astype(jnp.bfloat16)


def solution(mesh):
    in_specs = (
        P("seq", "mp"),
        P("seq", "mp"),
        P("seq", "mp"),
        P(None, "mp"),
        P(None, "mp"),
        P(None, "mp"),
        P("mp", None),
        P("seq", None),
        P("seq"),
        P(None, "mp"),
    )
    out_specs = P("seq", "mp")
    return jax.shard_map(
        on_device, mesh=mesh, in_specs=in_specs, out_specs=out_specs, check_vma=False
    )
```

profile of v0, /device:TPU:1, one launch (start us, length us, event | category | flops | bytes accessed | tf_op | source)
XLA Modules:
  0.0 185.6 jit_solution(1224696215609933354)
XLA Ops:
  8.8 4.6 %collective-permute-start = (bf16[512,256]{0,1:T(8,128)(2,1)}, bf16[512,256]{0,1:T(8,128)(2,1)}, u32[]{:S(2)}, u32[]{:S(2)}) collective-permute-start(bf16[512,256]{0,1:T(8,128)(2,1)} %slice.67), channel_id=1, source_target_pairs={{0,4},{4,8},{8,12},{12,16},{16,20},{20,24},{24,28},{1,5},{5,9},{9,... | collective-permute-start | bytes 786440 | tf_op jit(solution)/shard_map/ppermute | solution.py:14
  14.8 3.2 %collective-permute-start.1 = (bf16[512,256]{0,1:T(8,128)(2,1)S(1)}, bf16[512,256]{0,1:T(8,128)(2,1)}, u32[]{:S(2)}, u32[]{:S(2)}) collective-permute-start(bf16[512,256]{0,1:T(8,128)(2,1)S(1)} %slice.68), channel_id=1, source_target_pairs={{0,4},{4,8},{8,12},{12,16},{16,20},{20,24},{24,28},{1,5},{5,9},{9,... | collective-permute-start | bytes 786440 | tf_op jit(solution)/shard_map/ppermute | solution.py:14
  17.9 1.8 convolution_convert_fusion.1
  21.5 2.0 %collective-permute-done.1 = bf16[512,256]{0,1:T(8,128)(2,1)} collective-permute-done((bf16[512,256]{0,1:T(8,128)(2,1)S(1)}, bf16[512,256]{0,1:T(8,128)(2,1)}, u32[]{:S(2)}, u32[]{:S(2)}) %collective-permute-start.1) | collective-permute-done | bytes 262176 | tf_op jit(solution)/shard_map/ppermute | solution.py:14
  24.7 64.1 %while.16 = (s32[]{:T(128)}, bf16[2,512,256]{2,1,0:T(8,128)(2,1)}, f32[2,1024,256]{2,1,0:T(8,128)}, f32[2,1024,256]{2,1,0:T(8,128)}, s32[2]{0:T(128)S(1)}, /*ind...) while((s32[]{:T(128)}, bf16[2,512,256]{2,1,0:T(8,128)(2,1)}, ...), condition=%wide.region_4.5_spmd, body=%wide.region_0.4_spmd.sunk | while | flops 1372063232 | bytes 162323568 | solution.py:91
  28.5 5.4 %fusion.88 = (f32[4,512]{1,0:T(4,128)S(1)}, f32[4,512,1024]{2,1,0:T(8,128)}) fusion(pred[512,1024]{1,0:T(8,128)(4,1)S(1)} %fusion.87, bf16[512,4,64]{0,2,1:T(8,128)(2,1)S(1)} %bitcast.80, bf16[1024,4,64]{0,2,1:T(8,128)(2,1)S(1)} %bitcast.78), kind=kOutput, calls=%fused_computation.68.clone.1 | convolution fusion | flops 276825088 | bytes 9707520 | tf_op jit(solution)/shard_map/while/body/eval_jaxpr/sub | solution.py:38
  34.1 4.7 %multiply_reduce_fusion.2 = (f32[4,512]{1,0:T(4,128)S(1)}, f32[4,512,1024]{2,1,0:T(8,128)S(1)}) fusion(f32[4,512,1024]{2,1,0:T(8,128)} %get-tuple-element.249, f32[4,512]{1,0:T(4,128)S(1)} %get-tuple-element.250, bf16[512,4,64]{0,2,1:T(8,128)(2,1)S(1)} %bitcast.93, bf16[1024,4,64]{0,2,1:T(8,128)(2,1)S(1)} %bitcast.84), kind=kOutput, calls=%fused_computation.3.clone.1 | convolution fusion | flops 274724864 | bytes 17580032 | tf_op jit(solution)/shard_map/while/body/eval_jaxpr/ihd,jhd->hij/dot_general | solution.py:40
  41.4 2.0 %copy-done.2 = bf16[4,512,1024]{2,1,0:T(8,128)(2,1)} copy-done((bf16[4,512,1024]{2,1,0:T(8,128)(2,1)}, bf16[4,512,1024]{2,1,0:T(8,128)(2,1)S(1)}, u32[]{:S(2)}) %copy-start.2) | copy-done | bytes 4194328 | tf_op jit(solution)/shard_map/while
  44.6 5.3 %fusion.89 = f32[4,64,1024]{2,1,0:T(8,128)} fusion(bf16[512,4,64]{0,2,1:T(8,128)(2,1)S(1)} %bitcast.94, f32[4,512,1024]{2,1,0:T(8,128)} %get-tuple-element.249, f32[4,512]{1,0:T(4,128)S(1)} %get-tuple-element.250), kind=kOutput, calls=%fused_computation.7.clone.1 | convolution fusion | flops 272629760 | bytes 9707520 | tf_op jit(solution)/shard_map/while/body/eval_jaxpr/hij,ihd->jhd/dot_general | solution.py:53
  60.5 5.4 %fusion.88 = (f32[4,512]{1,0:T(4,128)S(1)}, f32[4,512,1024]{2,1,0:T(8,128)}) fusion(pred[512,1024]{1,0:T(8,128)(4,1)S(1)} %fusion.87, bf16[512,4,64]{0,2,1:T(8,128)(2,1)S(1)} %bitcast.80, bf16[1024,4,64]{0,2,1:T(8,128)(2,1)S(1)} %bitcast.78), kind=kOutput, calls=%fused_computation.68.clone.1 | convolution fusion | flops 276825088 | bytes 9707520 | tf_op jit(solution)/shard_map/while/body/eval_jaxpr/sub | solution.py:38
  66.2 4.7 %multiply_reduce_fusion.2 = (f32[4,512]{1,0:T(4,128)S(1)}, f32[4,512,1024]{2,1,0:T(8,128)S(1)}) fusion(f32[4,512,1024]{2,1,0:T(8,128)} %get-tuple-element.249, f32[4,512]{1,0:T(4,128)S(1)} %get-tuple-element.250, bf16[512,4,64]{0,2,1:T(8,128)(2,1)S(1)} %bitcast.93, bf16[1024,4,64]{0,2,1:T(8,128)(2,1)S(1)} %bitcast.84), kind=kOutput, calls=%fused_computation.3.clone.1 | convolution fusion | flops 274724864 | bytes 17580032 | tf_op jit(solution)/shard_map/while/body/eval_jaxpr/ihd,jhd->hij/dot_general | solution.py:40
  73.4 2.0 %copy-done.2 = bf16[4,512,1024]{2,1,0:T(8,128)(2,1)} copy-done((bf16[4,512,1024]{2,1,0:T(8,128)(2,1)}, bf16[4,512,1024]{2,1,0:T(8,128)(2,1)S(1)}, u32[]{:S(2)}) %copy-start.2) | copy-done | bytes 4194328 | tf_op jit(solution)/shard_map/while
  76.6 5.3 %fusion.89 = f32[4,64,1024]{2,1,0:T(8,128)} fusion(bf16[512,4,64]{0,2,1:T(8,128)(2,1)S(1)} %bitcast.94, f32[4,512,1024]{2,1,0:T(8,128)} %get-tuple-element.249, f32[4,512]{1,0:T(4,128)S(1)} %get-tuple-element.250), kind=kOutput, calls=%fused_computation.7.clone.1 | convolution fusion | flops 272629760 | bytes 9707520 | tf_op jit(solution)/shard_map/while/body/eval_jaxpr/hij,ihd->jhd/dot_general | solution.py:53
  88.8 2.6 %fusion.38 = (f32[2,512,256]{2,1,0:T(8,128)S(1)}, f32[2,512,256]{2,1,0:T(8,128)S(1)}, f32[2,512,256]{2,1,0:T(8,128)S(1)}, f32[2,512,256]{2,1,0:T(8,128)S(1)}) fusion(f32[2,1024,256]{2,1,0:T(8,128)} %get-tuple-element.124, f32[2,1024,256]{2,1,0:T(8,128)} %get-tuple-element.125), kind=kLoop, calls=%fused_computation.69 | loop fusion | bytes 8388608 | tf_op jit(solution)/shard_map/slice | solution.py:63
  94.9 2.7 %fusion.42 = f32[1024,1024]{1,0:T(8,128)} fusion(bf16[1024,256]{1,0:T(8,128)(2,1)S(1)} %bitcast.95, bf16[1024,256]{1,0:T(8,128)(2,1)S(1)} %copy-done.12), kind=kOutput, calls=%fused_computation.73 | convolution fusion | flops 536870912 | bytes 5242880 | tf_op jit(solution)/shard_map/dot_general | solution.py:114
  97.6 3.4 %collective-permute-done.2 = bf16[512,256]{1,0:T(8,128)(2,1)S(1)} collective-permute-done((bf16[512,256]{1,0:T(8,128)(2,1)S(1)}, bf16[512,256]{1,0:T(8,128)(2,1)S(1)}, u32[]{:S(2)}, u32[]{:S(2)}) %collective-permute-start.2) | collective-permute-done | bytes 262176 | tf_op jit(solution)/shard_map/ppermute | solution.py:14
  101.1 2.7 %fusion.27 = f32[1024,1024]{1,0:T(8,128)} fusion(bf16[1024,256]{1,0:T(8,128)(2,1)S(1)} %copy-done.13, bf16[512,256]{1,0:T(8,128)(2,1)S(1)} %fusion.23, bf16[512,256]{1,0:T(8,128)(2,1)S(1)} %get-tuple-element.176), kind=kOutput, calls=%fused_computation.57 | convolution fusion | flops 537919488 | bytes 5242880 | tf_op jit(solution)/shard_map/dot_general | solution.py:115
  103.8 2.8 %collective-permute-done.3 = bf16[512,256]{1,0:T(8,128)(2,1)S(1)} collective-permute-done((bf16[512,256]{1,0:T(8,128)(2,1)S(1)}, bf16[512,256]{1,0:T(8,128)(2,1)S(1)}, u32[]{:S(2)}, u32[]{:S(2)}) %collective-permute-start.3) | collective-permute-done | bytes 262176 | tf_op jit(solution)/shard_map/ppermute | solution.py:14
  106.7 2.7 %fusion.31 = f32[1024,1024]{1,0:T(8,128)} fusion(bf16[1024,256]{1,0:T(8,128)(2,1)S(1)} %copy-done.14, bf16[512,256]{1,0:T(8,128)(2,1)S(1)} %fusion.26, bf16[512,256]{1,0:T(8,128)(2,1)S(1)} %get-tuple-element.178), kind=kOutput, calls=%fused_computation.61 | convolution fusion | flops 537919488 | bytes 5242880 | tf_op jit(solution)/shard_map/dot_general | solution.py:116
  109.4 13.2 %scatter_custom_fusion = f32[512,1024]{1,0:T(8,128)} fusion(s32[1024]{0:T(1024)} %subtract_add_fusion, f32[1024,1024]{1,0:T(8,128)} %fusion.31, f32[1024,1024]{1,0:T(8,128)} %fusion.42, f32[1024,1024]{1,0:T(8,128)} %fusion.27, f32[]{:T(128)} %constant.66.clone.1), kind=kCustom, calls=%fused_computation.32 | custom fusion | flops 3145728 | bytes 14680576 | tf_op jit(solution)/shard_map/scatter-add | solution.py:118
  125.2 12.4 %collective-permute-done.4 = bf16[256,1024]{1,0:T(8,128)(2,1)S(1)} collective-permute-done((bf16[256,1024]{1,0:T(8,128)(2,1)S(1)}, bf16[256,1024]{1,0:T(8,128)(2,1)S(1)}, u32[]{:S(2)}, u32[]{:S(2)}) %collective-permute-start.4) | collective-permute-done | bytes 524320 | tf_op jit(solution)/shard_map/ppermute | solution.py:14
  137.6 2.2 %fusion.19 = bf16[256,1024]{1,0:T(8,128)(2,1)} fusion(f32[512,1024]{1,0:T(8,128)} %scatter_custom_fusion, bf16[256,1024]{1,0:T(8,128)(2,1)S(1)} %collective-permute-done.4), kind=kLoop, calls=%fused_computation.47 | loop fusion | flops 786432 | bytes 2097152 | tf_op jit(solution)/shard_map/convert_element_type | solution.py:121
  139.8 35.7 %all-reduce.6.cloned.1.call-done = bf16[256,1024]{1,0:T(8,128)(2,1)} async-done(((bf16[256,1024]{1,0:T(8,128)(2,1)}), bf16[256,1024]{1,0:T(8,128)(2,1)}) %all-reduce.6.cloned.1.call-update) | async-done | bytes 524304 | tf_op jit(solution)/shard_map/psum | solution.py:121
  175.5 3.3 %convolution_convert_fusion = bf16[256,1024]{1,0:T(8,128)(2,1)} fusion(bf16[256,1024]{1,0:T(8,128)(2,1)} %all-reduce.6.cloned.1.call-done, bf16[1024,1024]{1,0:T(8,128)(2,1)} %param.21), kind=kOutput, calls=%fused_computation.43 | convolution fusion | flops 537133056 | bytes 3145728 | tf_op jit(solution)/shard_map/dot_general | solution.py:122
  (126 shorter events, 38.9 us)
Async XLA Ops:
  6.5 11.4 %copy-start = (bf16[1024,1024]{1,0:T(8,128)(2,1)S(1)}, bf16[1024,1024]{1,0:T(8,128)(2,1)}, u32[]{:S(2)}) copy-start(bf16[1024,1024]{1,0:T(8,128)(2,1)} %param.19) | copy-start | bytes 6291460
  6.5 169.0 %all-reduce.6.cloned.1.call-start = ((), (), s32[]{:S(2)}) async-start(), calls=%async_computation | async-start | bytes 1048576 | tf_op jit(solution)/shard_map/psum | solution.py:121
  7.9 11.8 %copy-start.18 = (s32[1024]{0:T(1024)S(1)}, s32[1024]{0:T(1024)}, u32[]{:S(2)}) copy-start(s32[1024]{0:T(1024)} %param.20) | copy-start | bytes 12292
  8.8 11.5 %collective-permute-start = (bf16[512,256]{0,1:T(8,128)(2,1)}, bf16[512,256]{0,1:T(8,128)(2,1)}, u32[]{:S(2)}, u32[]{:S(2)}) collective-permute-start(bf16[512,256]{0,1:T(8,128)(2,1)} %slice.67), channel_id=1, source_target_pairs={{0,4},{4,8},{8,12},{12,16},{16,20},{20,24},{24,28},{1,5},{5,9},{9,... | collective-permute-start | bytes 786440 | tf_op jit(solution)/shard_map/ppermute | solution.py:14
  14.7 6.8 %copy-start.10 = (bf16[1024,256]{0,1:T(8,128)(2,1)}, bf16[1024,256]{0,1:T(8,128)(2,1)S(1)}, u32[]{:S(2)}) copy-start(bf16[1024,256]{0,1:T(8,128)(2,1)S(1)} %copy.19) | copy-start | bytes 1572868
  14.8 8.8 %collective-permute-start.1 = (bf16[512,256]{0,1:T(8,128)(2,1)S(1)}, bf16[512,256]{0,1:T(8,128)(2,1)}, u32[]{:S(2)}, u32[]{:S(2)}) collective-permute-start(bf16[512,256]{0,1:T(8,128)(2,1)S(1)} %slice.68), channel_id=1, source_target_pairs={{0,4},{4,8},{8,12},{12,16},{16,20},{20,24},{24,28},{1,5},{5,9},{9,... | collective-permute-start | bytes 786440 | tf_op jit(solution)/shard_map/ppermute | solution.py:14
  24.7 9.1 %copy-start.4 = (bf16[1536,256]{0,1:T(8,128)(2,1)}, bf16[1536,256]{0,1:T(8,128)(2,1)S(1)}, u32[]{:S(2)}) copy-start(bf16[1536,256]{0,1:T(8,128)(2,1)S(1)} %get-tuple-element.292) | copy-start | bytes 2359300 | tf_op jit(solution)/shard_map/while
  24.8 9.1 %copy-start.8 = (bf16[1024,256]{1,0:T(8,128)(2,1)}, bf16[1024,256]{1,0:T(8,128)(2,1)S(1)}, u32[]{:S(2)}) copy-start(bf16[1024,256]{1,0:T(8,128)(2,1)S(1)} %get-tuple-element.295) | copy-start | bytes 1572868 | tf_op jit(solution)/shard_map/while
  24.8 9.3 %copy-start.6 = (bf16[1536,256]{0,1:T(8,128)(2,1)}, bf16[1536,256]{0,1:T(8,128)(2,1)S(1)}, u32[]{:S(2)}) copy-start(bf16[1536,256]{0,1:T(8,128)(2,1)S(1)} %get-tuple-element.296) | copy-start | bytes 2359300 | tf_op jit(solution)/shard_map/while
  34.1 4.8 %slice-start = ((s8[8388608]{0:T(1024)(128)(4,1)}), s8[4194304]{0:T(1024)(128)(4,1)S(1)}, s32[]{:S(2)}) async-start(s8[8388608]{0:T(1024)(128)(4,1)} %bitcast.75), calls=%async_computation.1 | async-start | bytes 8388608 | tf_op jit(solution)/shard_map/while
  34.1 5.9 %slice-start.1 = ((s8[8388608]{0:T(1024)(128)(4,1)}), s8[4194304]{0:T(1024)(128)(4,1)S(1)}, s32[]{:S(2)}) async-start(s8[8388608]{0:T(1024)(128)(4,1)} %bitcast.75), calls=%async_computation.2 | async-start | bytes 8388608 | tf_op jit(solution)/shard_map/while
  51.5 4.5 %copy-start.15 = (bf16[2,512,256]{2,1,0:T(8,128)(2,1)S(1)}, bf16[2,512,256]{2,1,0:T(8,128)(2,1)}, u32[]{:S(2)}) copy-start(bf16[2,512,256]{2,1,0:T(8,128)(2,1)} %get-tuple-element.272) | copy-start | bytes 1572868 | tf_op jit(solution)/shard_map/while
  56.8 9.1 %copy-start.4 = (bf16[1536,256]{0,1:T(8,128)(2,1)}, bf16[1536,256]{0,1:T(8,128)(2,1)S(1)}, u32[]{:S(2)}) copy-start(bf16[1536,256]{0,1:T(8,128)(2,1)S(1)} %get-tuple-element.292) | copy-start | bytes 2359300 | tf_op jit(solution)/shard_map/while
  56.8 9.1 %copy-start.8 = (bf16[1024,256]{1,0:T(8,128)(2,1)}, bf16[1024,256]{1,0:T(8,128)(2,1)S(1)}, u32[]{:S(2)}) copy-start(bf16[1024,256]{1,0:T(8,128)(2,1)S(1)} %get-tuple-element.295) | copy-start | bytes 1572868 | tf_op jit(solution)/shard_map/while
  56.8 9.3 %copy-start.6 = (bf16[1536,256]{0,1:T(8,128)(2,1)}, bf16[1536,256]{0,1:T(8,128)(2,1)S(1)}, u32[]{:S(2)}) copy-start(bf16[1536,256]{0,1:T(8,128)(2,1)S(1)} %get-tuple-element.296) | copy-start | bytes 2359300 | tf_op jit(solution)/shard_map/while
  66.1 4.8 %slice-start = ((s8[8388608]{0:T(1024)(128)(4,1)}), s8[4194304]{0:T(1024)(128)(4,1)S(1)}, s32[]{:S(2)}) async-start(s8[8388608]{0:T(1024)(128)(4,1)} %bitcast.75), calls=%async_computation.1 | async-start | bytes 8388608 | tf_op jit(solution)/shard_map/while
  66.2 5.9 %slice-start.1 = ((s8[8388608]{0:T(1024)(128)(4,1)}), s8[4194304]{0:T(1024)(128)(4,1)S(1)}, s32[]{:S(2)}) async-start(s8[8388608]{0:T(1024)(128)(4,1)} %bitcast.75), calls=%async_computation.2 | async-start | bytes 8388608 | tf_op jit(solution)/shard_map/while
  83.5 4.5 %copy-start.15 = (bf16[2,512,256]{2,1,0:T(8,128)(2,1)S(1)}, bf16[2,512,256]{2,1,0:T(8,128)(2,1)}, u32[]{:S(2)}) copy-start(bf16[2,512,256]{2,1,0:T(8,128)(2,1)} %get-tuple-element.272) | copy-start | bytes 1572868 | tf_op jit(solution)/shard_map/while
  91.6 9.4 %collective-permute-start.2 = (bf16[512,256]{1,0:T(8,128)(2,1)S(1)}, bf16[512,256]{1,0:T(8,128)(2,1)S(1)}, u32[]{:S(2)}, u32[]{:S(2)}) collective-permute-start(bf16[512,256]{1,0:T(8,128)(2,1)S(1)} %get-tuple-element.177), channel_id=1, source_target_pairs={{4,0},{8,4},{12,8},{16,12},{20,16},{24,20},{28,24},{5,1},{9,5},{13... | collective-permute-start | bytes 786440 | tf_op jit(solution)/shard_map/ppermute | solution.py:14
  93.2 7.9 %copy-start.13 = (bf16[1024,256]{1,0:T(8,128)(2,1)S(1)}, bf16[1024,256]{1,0:T(8,128)(2,1)}, u32[]{:S(2)}) copy-start(bf16[1024,256]{1,0:T(8,128)(2,1)} %param.16) | copy-start | bytes 1572868
  93.2 13.4 %collective-permute-start.3 = (bf16[512,256]{1,0:T(8,128)(2,1)S(1)}, bf16[512,256]{1,0:T(8,128)(2,1)S(1)}, u32[]{:S(2)}, u32[]{:S(2)}) collective-permute-start(bf16[512,256]{1,0:T(8,128)(2,1)S(1)} %get-tuple-element.179), channel_id=1, source_target_pairs={{4,0},{8,4},{12,8},{16,12},{20,16},{24,20},{28,24},{5,1},{9,5},{13... | collective-permute-start | bytes 786440 | tf_op jit(solution)/shard_map/ppermute | solution.py:14
  101.1 5.6 %copy-start.14 = (bf16[1024,256]{1,0:T(8,128)(2,1)S(1)}, bf16[1024,256]{1,0:T(8,128)(2,1)}, u32[]{:S(2)}) copy-start(bf16[1024,256]{1,0:T(8,128)(2,1)} %param.17) | copy-start | bytes 1572868
  109.4 69.4 %copy-start.1 = (bf16[1024,1024]{1,0:T(8,128)(2,1)S(1)}, bf16[1024,1024]{1,0:T(8,128)(2,1)}, u32[]{:S(2)}) copy-start(bf16[1024,1024]{1,0:T(8,128)(2,1)} %param.19) | copy-start | bytes 6291460
  123.9 13.7 %collective-permute-start.4 = (bf16[256,1024]{1,0:T(8,128)(2,1)S(1)}, bf16[256,1024]{1,0:T(8,128)(2,1)S(1)}, u32[]{:S(2)}, u32[]{:S(2)}) collective-permute-start(bf16[256,1024]{1,0:T(8,128)(2,1)S(1)} %slice.103), channel_id=1, source_target_pairs={{4,0},{8,4},{12,8},{16,12},{20,16},{24,20},{28,24},{5,1},{9,5},{13... | collective-permute-start | bytes 1572872 | tf_op jit(solution)/shard_map/ppermute | solution.py:14
  (15 other events, 42.0 us)
Sparse Core Ops, SparseCore 0:
  139.9 35.5 all-reduce.5
where the time goes:
time: 188 us; the launch traced here: 186 us
  waiting for transfers between devices  56.4 us (30%)
  matrix products  48.5 us (26%)
  local copies, waits for them, and re-layouts  29.7 us (16%)
  other arithmetic  22.2 us (12%)
  between operations  13.6 us (7%)
  starting transfers between devices  12.1 us (6%)
  loops' own time  3.07 us (2%)
    psum x1, waiting for transfers between devices, on_device(): patch_low = lax.psum(owned.astype(jnp.bfloat16), 'mp')  35.7 us
    ppermute x5, waiting for transfers between devices, passed_along(): lax.ppermute(value, axis, [(source, source + steps) for source in range(l...  20.7 us
    scatter-add x1, other arithmetic, on_device(): frame = jax.ops.segment_sum(byte_grad, local_slot, num_segments=slots)  13.2 us
    ppermute x5, starting transfers between devices, passed_along(): lax.ppermute(value, axis, [(source, source + steps) for source in range(l...  12.1 us
    while x48, local copies, waits for them, and re-layouts  10.7 us
    sub x2, matrix products, block_grads(): raised = jnp.exp(scores - peak)  10.7 us
    dot_general x2, matrix products, block_grads(): jnp.einsum('hij,ihd->jhd', attend_low, grad_heads, preferred_element_type...  10.6 us
    dot_general x2, matrix products, block_grads(): jnp.einsum('ihd,jhd->hij', grad_heads, value_heads, preferred_element_typ...  9.47 us
  transfers between devices with their start and end apart: 6, of which 5 were waited for; matrix products, arithmetic and copies ran while one was open for 6% of the time, Pallas kernels for 0%

commit v1 on v0

v1 whole, which is shorter than its diff:
```python
import functools

import jax
import jax.numpy as jnp
from jax import lax
from jax.experimental import pallas as pl
from jax.experimental.pallas import tpu as pltpu
from jax.sharding import PartitionSpec as P

HS = 64
WINDOW = 512
PATCH_DEV = 256
BLOCK = 256
SPAN = WINDOW + BLOCK
MESH = pl.DeviceIdType.MESH
F32 = jnp.float32
BF16 = jnp.bfloat16


def dot_nt(a, b):
    return lax.dot_general(a, b, (((1,), (1,)), ((), ())), preferred_element_type=F32)


def dot_nn(a, b):
    return lax.dot_general(a, b, (((1,), (0,)), ((), ())), preferred_element_type=F32)


def kernel(
    shards,
    q_hbm,
    k_hbm,
    v_hbm,
    wq_hbm,
    wk_hbm,
    wv_hbm,
    wout_hbm,
    dout_hbm,
    index_ref,
    unpatch_hbm,
    out_ref,
    q,
    kx,
    vx,
    wq,
    wk,
    wv,
    wout,
    dout,
    unpatch,
    dk,
    dv,
    grads,
    p_low,
    ds_low,
    qb,
    gb,
    halo_index,
    prev,
    from_next,
    give,
    take,
    half,
    half_in,
    last,
    total,
    load_sem,
    halo_send,
    halo_recv,
    prev_send,
    prev_recv,
    core_send,
    core_recv,
    far_send,
    far_recv,
    near_send,
    near_recv,
):
    rows = q_hbm.shape[0]
    width = q_hbm.shape[1]
    heads = width // HS
    blocks = rows // BLOCK
    shard = lax.axis_index("seq")
    me = lax.axis_index("mp")
    core = lax.rem(me, 2)
    near = me + 1 - 2 * core
    far = lax.rem(me + 2, 4)
    has_prev = shard > 0
    has_next = shard < shards - 1

    loads = [
        pltpu.make_async_copy(src, dst, load_sem.at[n])
        for n, (src, dst) in enumerate(
            [
                (dout_hbm, dout),
                (wout_hbm, wout),
                (q_hbm, q),
                (k_hbm, kx.at[pl.ds(WINDOW, rows)]),
                (v_hbm, vx.at[pl.ds(WINDOW, rows)]),
                (wq_hbm, wq),
                (wk_hbm, wk),
                (wv_hbm, wv),
                (unpatch_hbm, unpatch),
            ]
        )
    ]
    for load in loads:
        load.start()

    barrier = pltpu.get_barrier_semaphore()
    for mate in (near, far):
        pl.semaphore_signal(barrier, inc=1, device_id=(shard, mate), device_id_type=MESH)

    @pl.when(has_prev)
    def _():
        pl.semaphore_signal(barrier, inc=1, device_id=(shard - 1, me), device_id_type=MESH)

    @pl.when(has_next)
    def _():
        pl.semaphore_signal(barrier, inc=1, device_id=(shard + 1, me), device_id_type=MESH)

    peers = 2 + has_prev.astype(jnp.int32) + has_next.astype(jnp.int32)
    pl.semaphore_wait(barrier, peers)

    def halo(n, src, dst):
        return pltpu.make_async_remote_copy(
            src_ref=src,
            dst_ref=dst,
            send_sem=halo_send.at[n],
            recv_sem=halo_recv.at[n],
            device_id=(shard + 1, me),
            device_id_type=MESH,
        )

    tail = rows - WINDOW
    late = pl.ds(BLOCK, BLOCK)
    early = pl.ds(0, BLOCK)
    halos = [
        halo(0, k_hbm.at[pl.ds(tail + BLOCK, BLOCK)], kx.at[late]),
        halo(1, v_hbm.at[pl.ds(tail + BLOCK, BLOCK)], vx.at[late]),
        halo(2, k_hbm.at[pl.ds(tail, BLOCK)], kx.at[early]),
        halo(3, v_hbm.at[pl.ds(tail, BLOCK)], vx.at[early]),
        halo(4, index_ref, halo_index),
    ]

    @pl.when(has_next)
    def _():
        for copy in halos:
            copy.start()

    @pl.when(shard == 0)
    def _():
        kx[pl.ds(0, WINDOW), :] = jnp.zeros((WINDOW, width), BF16)
        vx[pl.ds(0, WINDOW), :] = jnp.zeros((WINDOW, width), BF16)
        halo_index[...] = jnp.zeros_like(halo_index)

    dk[...] = jnp.zeros_like(dk)
    dv[...] = jnp.zeros_like(dv)
    for load in loads[:5]:
        load.wait()

    def one_hot(index_row, base):
        slot = lax.broadcasted_iota(jnp.int32, (PATCH_DEV, 128), 0)
        return jnp.where(slot == index_row - base, 1.0, 0.0).astype(BF16)

    lane_head = lax.broadcasted_iota(jnp.int32, (BLOCK, width), 1) // HS

    prev_copy = pltpu.make_async_remote_copy(
        src_ref=prev,
        dst_ref=from_next,
        send_sem=prev_send,
        recv_sem=prev_recv,
        device_id=(shard - 1, me),
        device_id_type=MESH,
    )

    def send_prev():
        base = (shard - 1) * PATCH_DEV
        halo_rows = 4
        hot = jnp.concatenate(
            [one_hot(halo_index[pl.ds(4 + c, 1), :], base) for c in range(halo_rows)]
            + [one_hot(index_ref[pl.ds(0, 1), :], base)],
            axis=1,
        )
        span = pl.ds(0, WINDOW + 128)
        prev[:, pl.ds(0, width)] = dot_nn(
            hot[:, WINDOW:], grads[pl.ds(0, 128), pl.ds(0, width)]
        ).astype(BF16)
        prev[:, pl.ds(width, width)] = dot_nn(hot, dk[span, :].astype(BF16)).astype(BF16)
        prev[:, pl.ds(2 * width, width)] = dot_nn(hot, dv[span, :].astype(BF16)).astype(BF16)
        prev_copy.start()

    def one_block(step, carry):
        block = jnp.where(step < 3, 2 - step, 3)
        start = pl.multiple_of(block * BLOCK, BLOCK)

        @pl.when((step == 1) & has_prev)
        def _():
            halos[0].wait_recv()
            halos[1].wait_recv()

        @pl.when((step == 2) & has_prev)
        def _():
            halos[2].wait_recv()
            halos[3].wait_recv()
            halos[4].wait_recv()

        @pl.when((step == 3) & has_prev)
        def _():
            send_prev()

        span = pl.ds(start, SPAN)
        mine = pl.ds(start, BLOCK)
        q_block = (q[mine, :].astype(F32) * HS**-0.5).astype(BF16)
        g_block = dot_nt(dout[mine, :], wout[...]).astype(BF16)
        for h in range(heads):
            keep = lane_head == h
            qb[pl.ds(h * BLOCK, BLOCK), :] = jnp.where(keep, q_block, jnp.zeros_like(q_block))
            gb[pl.ds(h * BLOCK, BLOCK), :] = jnp.where(keep, g_block, jnp.zeros_like(g_block))
        keys = kx[span, :]
        values = vx[span, :]
        keys_t = keys.T
        blocked = jnp.where(shard == 0, jnp.maximum(WINDOW - start, 0), 0)
        key_pos = lax.broadcasted_iota(jnp.int32, (SPAN, BLOCK), 0)
        query_pos = lax.broadcasted_iota(jnp.int32, (SPAN, BLOCK), 1)
        allowed = (key_pos > query_pos) & (key_pos <= query_pos + WINDOW) & (key_pos >= blocked)
        d_query = []
        for h in range(heads):
            head = pl.ds(h * BLOCK, BLOCK)
            scores = jnp.where(allowed, dot_nt(keys, qb[head, :]), -1e30)
            peak = jnp.max(scores, axis=0, keepdims=True)
            raised = jnp.exp(scores - peak)
            d_attend = dot_nt(values, gb[head, :])
            inverse = 1.0 / jnp.sum(raised, axis=0, keepdims=True)
            row_dot = jnp.sum(raised * d_attend, axis=0, keepdims=True) * inverse
            attend = raised * inverse
            d_scores = (attend * (d_attend - row_dot)).astype(BF16)
            p_low[:, head] = attend.astype(BF16)
            ds_low[:, head] = d_scores
            d_query.append(dot_nn(keys_t[h * HS : (h + 1) * HS, :], d_scores))
        dk[span, :] += dot_nn(ds_low[...], qb[...])
        dv[span, :] += dot_nn(p_low[...], gb[...])
        d_query = jnp.concatenate(d_query, axis=0) * HS**-0.5
        grads[mine, pl.ds(0, width)] = d_query.T.astype(BF16)
        return carry

    lax.fori_loop(0, blocks, one_block, 0)

    grads[:, pl.ds(width, width)] = dk[pl.ds(WINDOW, rows), :].astype(BF16)
    grads[:, pl.ds(2 * width, width)] = dv[pl.ds(WINDOW, rows), :].astype(BF16)
    hot = jnp.concatenate(
        [one_hot(index_ref[pl.ds(c, 1), :], shard * PATCH_DEV) for c in range(rows // 128)],
        axis=1,
    )
    pooled = dot_nn(hot, grads[...])
    for load in loads[5:]:
        load.wait()

    total[...] = pooled

    @pl.when(has_next)
    def _():
        prev_copy.wait_recv()
        total[...] += from_next[...].astype(F32)

    def project(first):
        part = total[pl.ds(first, PATCH_DEV // 2), :].astype(BF16)
        return (
            dot_nt(part[:, :width], wq[...])
            + dot_nt(part[:, width : 2 * width], wk[...])
            + dot_nt(part[:, 2 * width :], wv[...])
        )

    side = PATCH_DEV // 2
    give[...] = project(pl.multiple_of((1 - core) * side, side)).astype(BF16)
    core_copy = pltpu.make_async_remote_copy(
        src_ref=give,
        dst_ref=take,
        send_sem=core_send,
        recv_sem=core_recv,
        device_id=(shard, near),
        device_id_type=MESH,
    )
    core_copy.start()
    kept = project(pl.multiple_of(core * side, side))
    core_copy.wait_recv()
    kept = kept + take[...].astype(F32)
    half[...] = kept.astype(BF16)
    far_copy = pltpu.make_async_remote_copy(
        src_ref=half,
        dst_ref=half_in,
        send_sem=far_send,
        recv_sem=far_recv,
        device_id=(shard, far),
        device_id_type=MESH,
    )
    far_copy.start()
    far_copy.wait_recv()
    give_back = (kept + half_in[...].astype(F32)).astype(BF16)
    core_copy.wait_send()
    give[...] = give_back
    near_copy = pltpu.make_async_remote_copy(
        src_ref=give,
        dst_ref=last,
        send_sem=near_send,
        recv_sem=near_recv,
        device_id=(shard, near),
        device_id_type=MESH,
    )
    near_copy.start()
    out_ref[pl.ds(pl.multiple_of(core * side, side), side), :] = dot_nn(
        give[...], unpatch[...]
    ).astype(BF16)
    near_copy.wait_recv()
    out_ref[pl.ds(pl.multiple_of((1 - core) * side, side), side), :] = dot_nn(
        last[...], unpatch[...]
    ).astype(BF16)
    near_copy.wait_send()
    far_copy.wait_send()

    @pl.when(has_prev)
    def _():
        prev_copy.wait_send()

    @pl.when(has_next)
    def _():
        for copy in halos:
            copy.wait_send()


def on_device(
    shards,
    queries,
    byte_keys,
    byte_values,
    w_query,
    w_key,
    w_value,
    w_out,
    d_output,
    patch_index,
    unpatch,
):
    rows, width = queries.shape
    full = w_query.shape[0]
    out_width = unpatch.shape[1]
    heads = width // HS
    side = PATCH_DEV // 2
    vmem = pltpu.VMEM
    dma = pltpu.SemaphoreType.DMA
    anywhere = pl.BlockSpec(memory_space=pl.ANY)
    local = pl.BlockSpec(memory_space=pltpu.VMEM)
    return pl.pallas_call(
        functools.partial(kernel, shards),
        out_shape=jax.ShapeDtypeStruct((PATCH_DEV, out_width), BF16),
        in_specs=[anywhere] * 8 + [local, anywhere],
        out_specs=local,
        scratch_shapes=[
            vmem((rows, width), BF16),
            vmem((rows + WINDOW, width), BF16),
            vmem((rows + WINDOW, width), BF16),
            vmem(w_query.shape, BF16),
            vmem(w_key.shape, BF16),
            vmem(w_value.shape, BF16),
            vmem(w_out.shape, BF16),
            vmem(d_output.shape, BF16),
            vmem(unpatch.shape, BF16),
            vmem((rows + WINDOW, width), F32),
            vmem((rows + WINDOW, width), F32),
            vmem((rows, 3 * width), BF16),
            vmem((SPAN, heads * BLOCK), BF16),
            vmem((SPAN, heads * BLOCK), BF16),
            vmem((heads * BLOCK, width), BF16),
            vmem((heads * BLOCK, width), BF16),
            vmem((8, 128), jnp.int32),
            vmem((PATCH_DEV, 3 * width), BF16),
            vmem((PATCH_DEV, 3 * width), BF16),
            vmem((side, full), BF16),
            vmem((side, full), BF16),
            vmem((side, full), BF16),
            vmem((side, full), BF16),
            vmem((side, full), BF16),
            vmem((PATCH_DEV, 3 * width), F32),
            dma((9,)),
            dma((5,)),
            dma((5,)),
            dma,
            dma,
            dma,
            dma,
            dma,
            dma,
            dma,
            dma,
        ],
        compiler_params=pltpu.CompilerParams(
            collective_id=0, has_side_effects=True, vmem_limit_bytes=56 * 1024 * 1024
        ),
        name="fused_backward",
    )(
        queries,
        byte_keys,
        byte_values,
        w_query,
        w_key,
        w_value,
        w_out,
        d_output,
        patch_index.reshape(8, 128),
        unpatch,
    )


def solution(mesh):
    in_specs = (
        P("seq", "mp"),
        P("seq", "mp"),
        P("seq", "mp"),
        P(None, "mp"),
        P(None, "mp"),
        P(None, "mp"),
        P("mp", None),
        P("seq", None),
        P("seq"),
        P(None, "mp"),
    )
    return jax.shard_map(
        functools.partial(on_device, mesh.shape["seq"]),
        mesh=mesh,
        in_specs=in_specs,
        out_specs=P("seq", "mp"),
        check_vma=False,
    )
```

time: 188 us -> 45.7 us (0.24); the launches traced: 186 us -> 45.3 us
  waiting for transfers between devices: 56.4 us -> 0 us
  matrix products: 48.5 us -> 0 us
  Pallas kernels: 0 us -> 43.4 us
  local copies, waits for them, and re-layouts: 29.7 us -> 1.87 us
  other arithmetic: 22.2 us -> 0 us
  between operations: 13.6 us -> 0.01 us
  starting transfers between devices: 12.1 us -> 0 us
  loops' own time: 3.07 us -> 0 us
    pallas_call x0 -> x1, Pallas kernels: none -> 43.4 us  [on_device(): pl.pallas_call(functools.partial(kernel, shards), out_shape=jax.ShapeDtyp...]
    dot_general x13 -> x0, matrix products: 37.8 us -> none  [the longest x2 10.6 us: block_grads(): jnp.einsum('hij,ihd->jhd', attend_low, grad_heads, preferred_element_type...]
    psum x1 -> x0, waiting for transfers between devices: 35.7 us -> none  [on_device(): patch_low = lax.psum(owned.astype(jnp.bfloat16), 'mp')]
    ppermute x5 -> x0, waiting for transfers between devices: 20.7 us -> none  [passed_along(): lax.ppermute(value, axis, [(source, source + steps) for source in range(l...]
    scatter-add x1 -> x0, other arithmetic: 13.2 us -> none  [on_device(): frame = jax.ops.segment_sum(byte_grad, local_slot, num_segments=slots)]
    ppermute x5 -> x0, starting transfers between devices: 12.1 us -> none  [passed_along(): lax.ppermute(value, axis, [(source, source + steps) for source in range(l...]
    while x48 -> x0, local copies, waits for them, and re-layouts: 10.7 us -> none
    sub x2 -> x0, matrix products: 10.7 us -> none  [block_grads(): raised = jnp.exp(scores - peak)]
  transfers between devices with their start and end apart: 6 -> 0, of which waited for: 5 -> 0; matrix products, arithmetic and copies ran while one was open for 6% -> 0% of each run, Pallas kernels for 0% -> 0%
where the time goes in v1:
time: 45.7 us; the launch traced here: 45.3 us
  Pallas kernels  43.4 us (95%)
  local copies, waits for them, and re-layouts  1.87 us (4%)
    pallas_call x1, Pallas kernels, on_device(): pl.pallas_call(functools.partial(kernel, shards), out_shape=jax.ShapeDtyp...  43.4 us
    unnamed x1, local copies, waits for them, and re-layouts  1.87 us

profile of v1, /device:TPU:1, one launch (start us, length us, event | category | flops | bytes accessed | tf_op | source)
XLA Modules:
  0.0 45.3 jit_solution(3778663510799064207)
XLA Ops:
  0.0 43.4 %fused_backward.1 = bf16[256,1024]{1,0:T(8,128)(2,1)} custom-call(bf16[1024,256]{1,0:T(8,128)(2,1)} %q_hbm.1, bf16[1024,256]{1,0:T(8,128)(2,1)} %k_hbm.1, bf16[1024,256]{1,0:T(8,128)(2,1)} %v_hbm.1, bf16[1024,256]{1,0:T(8,128)(2,1)} %wq_hbm.1, bf16[1024,256]{1,0:T(8,128)(2,1)} %wk_hbm.1, bf16[1024,256]{1,0:T(8,128)(2,1)} %wv_hbm.1, ...), custom_call_target="tpu_custom_call" | custom-call | tf_op jit(solution)/shard_map/fused_backward/pallas_call | solution.py:352
  43.5 1.9 %copy.12 = bf16[256,1024]{1,0:T(8,128)(2,1)} copy(bf16[256,1024]{1,0:T(8,128)(2,1)} %fused_backward.1) | data formatting | bytes 1048576

commit v2 on v1

v2 whole, which is shorter than its diff:
```python
import functools

import jax
import jax.numpy as jnp
from jax import lax
from jax.experimental import pallas as pl
from jax.experimental.pallas import tpu as pltpu
from jax.sharding import PartitionSpec as P

HS = 64
WINDOW = 512
PATCH_DEV = 256
BLOCK = 256
CHUNK = 128
SPAN = WINDOW + CHUNK
PAIR = 2 * HS
PARTS = 4
MESH = pl.DeviceIdType.MESH
F32 = jnp.float32
BF16 = jnp.bfloat16


def dot_nt(a, b):
    return lax.dot_general(a, b, (((1,), (1,)), ((), ())), preferred_element_type=F32)


def dot_nn(a, b):
    return lax.dot_general(a, b, (((1,), (0,)), ((), ())), preferred_element_type=F32)


def kernel(
    shards,
    q_hbm,
    k_hbm,
    v_hbm,
    wq_hbm,
    wk_hbm,
    wv_hbm,
    wout_hbm,
    dout_hbm,
    index_ref,
    unpatch_hbm,
    out_ref,
    q,
    kx,
    vx,
    wq,
    wk,
    wv,
    wout,
    dout,
    unpatch,
    g,
    dk,
    dv,
    grads,
    halo_index,
    prev,
    from_next,
    give,
    take,
    half,
    half_in,
    done,
    last,
    kept,
    total,
    load_sem,
    halo_send,
    halo_recv,
    prev_send,
    prev_recv,
    core_send,
    core_recv,
    far_send,
    far_recv,
    near_send,
    near_recv,
):
    rows = q_hbm.shape[0]
    width = q_hbm.shape[1]
    pairs = width // PAIR
    shard = lax.axis_index("seq")
    me = lax.axis_index("mp")
    core = lax.rem(me, 2)
    near = me + 1 - 2 * core
    far = lax.rem(me + 2, 4)
    has_prev = shard > 0
    has_next = shard < shards - 1

    def lanes(pair):
        return pl.ds(pair * PAIR, PAIR)

    own = pl.ds(WINDOW, rows)
    moves = [(dout_hbm, dout), (wout_hbm, wout)]
    for pair in range(pairs):
        moves += [
            (q_hbm.at[:, lanes(pair)], q.at[pair]),
            (k_hbm.at[:, lanes(pair)], kx.at[pair, own]),
            (v_hbm.at[:, lanes(pair)], vx.at[pair, own]),
        ]
    soon = len(moves)
    moves += [(wq_hbm, wq), (wk_hbm, wk), (wv_hbm, wv), (unpatch_hbm, unpatch)]
    loads = [
        pltpu.make_async_copy(src, dst, load_sem.at[n]) for n, (src, dst) in enumerate(moves)
    ]
    for load in loads:
        load.start()

    barrier = pltpu.get_barrier_semaphore()
    for mate in (near, far):
        pl.semaphore_signal(barrier, inc=1, device_id=(shard, mate), device_id_type=MESH)

    @pl.when(has_prev)
    def _():
        pl.semaphore_signal(barrier, inc=1, device_id=(shard - 1, me), device_id_type=MESH)

    @pl.when(has_next)
    def _():
        pl.semaphore_signal(barrier, inc=1, device_id=(shard + 1, me), device_id_type=MESH)

    peers = 2 + has_prev.astype(jnp.int32) + has_next.astype(jnp.int32)
    pl.semaphore_wait(barrier, peers)

    def halo(n, src, dst):
        return pltpu.make_async_remote_copy(
            src_ref=src,
            dst_ref=dst,
            send_sem=halo_send.at[n],
            recv_sem=halo_recv.at[n],
            device_id=(shard + 1, me),
            device_id_type=MESH,
        )

    tail = rows - WINDOW
    halos = [halo(0, index_ref, halo_index)]
    for pair in range(pairs):
        for first in (BLOCK, 0):
            for src, dst in ((k_hbm, kx), (v_hbm, vx)):
                halos.append(
                    halo(
                        len(halos),
                        src.at[pl.ds(tail + first, BLOCK), lanes(pair)],
                        dst.at[pair, pl.ds(first, BLOCK)],
                    )
                )

    @pl.when(has_next)
    def _():
        for copy in halos:
            copy.start()

    @pl.when(shard == 0)
    def _():
        kx[:, pl.ds(0, WINDOW), :] = jnp.zeros((pairs, WINDOW, PAIR), BF16)
        vx[:, pl.ds(0, WINDOW), :] = jnp.zeros((pairs, WINDOW, PAIR), BF16)
        halo_index[...] = jnp.zeros_like(halo_index)

    dk[...] = jnp.zeros_like(dk)
    dv[...] = jnp.zeros_like(dv)
    for load in loads[:soon]:
        load.wait()

    def output_grads(block, carry):
        mine = pl.ds(pl.multiple_of(block * BLOCK, BLOCK), BLOCK)
        heads_grad = dot_nt(dout[mine, :], wout[...]).astype(BF16)
        for pair in range(pairs):
            g[pair, mine, :] = heads_grad[:, pair * PAIR : (pair + 1) * PAIR]
        return carry

    lax.fori_loop(0, rows // BLOCK, output_grads, 0)

    def one_hot(index_row, base):
        slot = lax.broadcasted_iota(jnp.int32, (PATCH_DEV, 128), 0)
        return jnp.where(slot == index_row - base, 1.0, 0.0).astype(BF16)

    first_head = lax.broadcasted_iota(jnp.int32, (CHUNK, PAIR), 1) < HS

    def by_head(rows_of):
        blank = jnp.zeros_like(rows_of)
        return jnp.concatenate(
            [jnp.where(first_head, rows_of, blank), jnp.where(first_head, blank, rows_of)], axis=0
        )

    prev_copies = [
        pltpu.make_async_remote_copy(
            src_ref=prev.at[pair],
            dst_ref=from_next.at[pair],
            send_sem=prev_send.at[pair],
            recv_sem=prev_recv.at[pair],
            device_id=(shard - 1, me),
            device_id_type=MESH,
        )
        for pair in range(pairs)
    ]

    def send_prev(pair):
        base = (shard - 1) * PATCH_DEV
        hot = jnp.concatenate(
            [one_hot(halo_index[pl.ds(4 + c, 1), :], base) for c in range(WINDOW // 128)]
            + [one_hot(index_ref[pl.ds(0, 1), :], base)],
            axis=1,
        )
        span = pl.ds(0, WINDOW + 128)
        prev[pair, :, pl.ds(0, PAIR)] = dot_nn(
            hot[:, WINDOW:], grads[pl.ds(0, 128), lanes(pair)]
        ).astype(BF16)
        terms = jnp.concatenate([dk[pair, span, :], dv[pair, span, :]], axis=1).astype(BF16)
        prev[pair, :, pl.ds(PAIR, 2 * PAIR)] = dot_nn(hot, terms).astype(BF16)
        prev_copies[pair].start()

    top_key = lax.broadcasted_iota(jnp.int32, (CHUNK, 2 * CHUNK), 0)
    query_pos = lax.rem(lax.broadcasted_iota(jnp.int32, (CHUNK, 2 * CHUNK), 1), CHUNK)
    middle_key = lax.broadcasted_iota(jnp.int32, (WINDOW - CHUNK, 2 * CHUNK), 0) + CHUNK

    def one_step(step, carry):
        block = jnp.where(step < 2, 2, jnp.where(step < 6, 1 - lax.rem(step, 2), 3))
        pair = jnp.where((step >= 2) & (step < 6), (step - 2) // 2, lax.rem(step, 2))

        for n in range(4):

            @pl.when((step == 2 + n) & has_prev)
            def _(n=n):
                if n == 0:
                    halos[0].wait_recv()
                halos[1 + 2 * n].wait_recv()
                halos[2 + 2 * n].wait_recv()

        for n in range(pairs):

            @pl.when((step == 4 + 2 * n) & has_prev)
            def _(n=n):
                send_prev(n)

        column = pl.ds(pl.multiple_of(pair * PAIR, PAIR), PAIR)
        results = []
        for c in range(BLOCK // CHUNK):
            start = pl.multiple_of(block * BLOCK + c * CHUNK, CHUNK)
            span = pl.ds(start, SPAN)
            mine = pl.ds(start, CHUNK)
            queries = by_head((q[pair, mine, :].astype(F32) * HS**-0.5).astype(BF16))
            grads_in = by_head(g[pair, mine, :])
            keys = kx[pair, span, :]
            values = vx[pair, span, :]
            blocked = jnp.where(shard == 0, jnp.maximum(WINDOW - start, 0), 0)
            scores = dot_nt(keys, queries)
            scores = jnp.concatenate(
                [
                    jnp.where(
                        top_key > jnp.maximum(query_pos, blocked - 1), scores[:CHUNK], -1e30
                    ),
                    jnp.where(middle_key >= blocked, scores[CHUNK:WINDOW], -1e30),
                    jnp.where(top_key <= query_pos, scores[WINDOW:], -1e30),
                ],
                axis=0,
            )
            peak = jnp.max(scores, axis=0, keepdims=True)
            raised = jnp.exp(scores - peak)
            d_attend = dot_nt(values, grads_in)
            inverse = 1.0 / jnp.sum(raised, axis=0, keepdims=True)
            row_dot = jnp.sum(raised * d_attend, axis=0, keepdims=True) * inverse
            attend = raised * inverse
            d_scores = (attend * (d_attend - row_dot)).astype(BF16)
            d_query = dot_nn(keys.T, d_scores) * HS**-0.5
            d_query = jnp.concatenate([d_query[:HS, :CHUNK], d_query[HS:, CHUNK:]], axis=0)
            results.append(
                (
                    span,
                    mine,
                    d_query.T.astype(BF16),
                    dot_nn(d_scores, queries),
                    dot_nn(attend.astype(BF16), grads_in),
                )
            )
        for span, mine, d_query, d_key, d_value in results:
            grads[mine, column] = d_query
            dk[pair, span, :] += d_key
            dv[pair, span, :] += d_value
        return carry

    lax.fori_loop(0, rows // BLOCK * pairs, one_step, 0)

    for pair in range(pairs):
        grads[:, pl.ds(width + pair * PAIR, PAIR)] = dk[pair, own, :].astype(BF16)
        grads[:, pl.ds(2 * width + pair * PAIR, PAIR)] = dv[pair, own, :].astype(BF16)
    hot = jnp.concatenate(
        [one_hot(index_ref[pl.ds(c, 1), :], shard * PATCH_DEV) for c in range(rows // 128)],
        axis=1,
    )
    pooled = dot_nn(hot, grads[...])
    for load in loads[soon:]:
        load.wait()

    total[...] = pooled

    @pl.when(has_next)
    def _():
        for pair in range(pairs):
            prev_copies[pair].wait_recv()
            for n in range(3):
                total[:, pl.ds(n * width + pair * PAIR, PAIR)] += from_next[
                    pair, :, pl.ds(n * PAIR, PAIR)
                ].astype(F32)

    def project(first):
        part = total[pl.ds(first, PATCH_DEV // 2), :].astype(BF16)
        return (
            dot_nt(part[:, :width], wq[...])
            + dot_nt(part[:, width : 2 * width], wk[...])
            + dot_nt(part[:, 2 * width :], wv[...])
        )

    side = PATCH_DEV // 2
    part = side // PARTS

    def swap(src, dst, sends, recvs, mate):
        return [
            pltpu.make_async_remote_copy(
                src_ref=src.at[pl.ds(n * part, part)],
                dst_ref=dst.at[pl.ds(n * part, part)],
                send_sem=sends.at[n],
                recv_sem=recvs.at[n],
                device_id=(shard, mate),
                device_id_type=MESH,
            )
            for n in range(PARTS)
        ]

    core_copies = swap(give, take, core_send, core_recv, near)
    far_copies = swap(half, half_in, far_send, far_recv, far)
    near_copies = swap(done, last, near_send, near_recv, near)
    give[...] = project(pl.multiple_of((1 - core) * side, side)).astype(BF16)
    for copy in core_copies:
        copy.start()
    kept[...] = project(pl.multiple_of(core * side, side))
    for n in range(PARTS):
        piece = pl.ds(n * part, part)
        core_copies[n].wait_recv()
        kept[piece, :] += take[piece, :].astype(F32)
        half[piece, :] = kept[piece, :].astype(BF16)
        far_copies[n].start()
    for n in range(PARTS):
        piece = pl.ds(n * part, part)
        far_copies[n].wait_recv()
        done[piece, :] = (kept[piece, :] + half_in[piece, :].astype(F32)).astype(BF16)
        near_copies[n].start()
    out_ref[pl.ds(pl.multiple_of(core * side, side), side), :] = dot_nn(
        done[...], unpatch[...]
    ).astype(BF16)
    for copy in near_copies:
        copy.wait_recv()
    out_ref[pl.ds(pl.multiple_of((1 - core) * side, side), side), :] = dot_nn(
        last[...], unpatch[...]
    ).astype(BF16)
    for copy in core_copies + far_copies + near_copies:
        copy.wait_send()

    @pl.when(has_prev)
    def _():
        for copy in prev_copies:
            copy.wait_send()

    @pl.when(has_next)
    def _():
        for copy in halos:
            copy.wait_send()


def on_device(
    shards,
    queries,
    byte_keys,
    byte_values,
    w_query,
    w_key,
    w_value,
    w_out,
    d_output,
    patch_index,
    unpatch,
):
    rows, width = queries.shape
    full = w_query.shape[0]
    out_width = unpatch.shape[1]
    pairs = width // PAIR
    side = PATCH_DEV // 2
    vmem = pltpu.VMEM
    dma = pltpu.SemaphoreType.DMA
    anywhere = pl.BlockSpec(memory_space=pl.ANY)
    local = pl.BlockSpec(memory_space=pltpu.VMEM)
    return pl.pallas_call(
        functools.partial(kernel, shards),
        out_shape=jax.ShapeDtypeStruct((PATCH_DEV, out_width), BF16),
        in_specs=[anywhere] * 8 + [local, anywhere],
        out_specs=local,
        scratch_shapes=[
            vmem((pairs, rows, PAIR), BF16),
            vmem((pairs, rows + WINDOW, PAIR), BF16),
            vmem((pairs, rows + WINDOW, PAIR), BF16),
            vmem(w_query.shape, BF16),
            vmem(w_key.shape, BF16),
            vmem(w_value.shape, BF16),
            vmem(w_out.shape, BF16),
            vmem(d_output.shape, BF16),
            vmem(unpatch.shape, BF16),
            vmem((pairs, rows, PAIR), BF16),
            vmem((pairs, rows + WINDOW, PAIR), F32),
            vmem((pairs, rows + WINDOW, PAIR), F32),
            vmem((rows, 3 * width), BF16),
            vmem((8, 128), jnp.int32),
            vmem((pairs, PATCH_DEV, 3 * PAIR), BF16),
            vmem((pairs, PATCH_DEV, 3 * PAIR), BF16),
            vmem((side, full), BF16),
            vmem((side, full), BF16),
            vmem((side, full), BF16),
            vmem((side, full), BF16),
            vmem((side, full), BF16),
            vmem((side, full), BF16),
            vmem((side, full), F32),
            vmem((PATCH_DEV, 3 * width), F32),
            dma((6 + 3 * pairs,)),
            dma((1 + 4 * pairs,)),
            dma((1 + 4 * pairs,)),
            dma((pairs,)),
            dma((pairs,)),
            dma((PARTS,)),
            dma((PARTS,)),
            dma((PARTS,)),
            dma((PARTS,)),
            dma((PARTS,)),
            dma((PARTS,)),
        ],
        compiler_params=pltpu.CompilerParams(
            collective_id=0, has_side_effects=True, vmem_limit_bytes=56 * 1024 * 1024
        ),
        name="fused_backward",
    )(
        queries,
        byte_keys,
        byte_values,
        w_query,
        w_key,
        w_value,
        w_out,
        d_output,
        patch_index.reshape(8, 128),
        unpatch,
    )


def solution(mesh):
    in_specs = (
        P("seq", "mp"),
        P("seq", "mp"),
        P("seq", "mp"),
        P(None, "mp"),
        P(None, "mp"),
        P(None, "mp"),
        P("mp", None),
        P("seq", None),
        P("seq"),
        P(None, "mp"),
    )
    return jax.shard_map(
        functools.partial(on_device, mesh.shape["seq"]),
        mesh=mesh,
        in_specs=in_specs,
        out_specs=P("seq", "mp"),
        check_vma=False,
    )
```

time: 45.7 us -> 40.3 us (0.88)
  Pallas kernels: 43.4 us -> 38.3 us
    pallas_call x1, Pallas kernels: 43.4 us -> 38.3 us  [on_device(): pl.pallas_call(functools.partial(kernel, shards), out_shape=jax.ShapeDtyp...]
where the time goes in v2:
time: 40.3 us; the launch traced here: 40.1 us
  Pallas kernels  38.3 us (95%)
  local copies, waits for them, and re-layouts  1.87 us (5%)
    pallas_call x1, Pallas kernels, on_device(): pl.pallas_call(functools.partial(kernel, shards), out_shape=jax.ShapeDtyp...  38.3 us
    unnamed x1, local copies, waits for them, and re-layouts  1.87 us

profile of v2, /device:TPU:1, one launch (start us, length us, event | category | flops | bytes accessed | tf_op | source)
XLA Modules:
  0.0 40.1 jit_solution(3074701024604967690)
XLA Ops:
  0.0 38.3 %fused_backward.1 = bf16[256,1024]{1,0:T(8,128)(2,1)} custom-call(bf16[1024,256]{1,0:T(8,128)(2,1)} %q_hbm.1, bf16[1024,256]{1,0:T(8,128)(2,1)} %k_hbm.1, bf16[1024,256]{1,0:T(8,128)(2,1)} %v_hbm.1, bf16[1024,256]{1,0:T(8,128)(2,1)} %wq_hbm.1, bf16[1024,256]{1,0:T(8,128)(2,1)} %wk_hbm.1, bf16[1024,256]{1,0:T(8,128)(2,1)} %wv_hbm.1, ...), custom_call_target="tpu_custom_call" | custom-call | tf_op jit(solution)/shard_map/fused_backward/pallas_call | solution.py:391
  38.3 1.9 %copy.12 = bf16[256,1024]{1,0:T(8,128)(2,1)} copy(bf16[256,1024]{1,0:T(8,128)(2,1)} %fused_backward.1) | data formatting | bytes 1048576

commit v3 on v2

--- a/solution.py
+++ b/solution.py
@@ -213,33 +213,35 @@
     query_pos = lax.rem(lax.broadcasted_iota(jnp.int32, (CHUNK, 2 * CHUNK), 1), CHUNK)
     middle_key = lax.broadcasted_iota(jnp.int32, (WINDOW - CHUNK, 2 * CHUNK), 0) + CHUNK
 
+    def column(row):
+        return jnp.broadcast_to(row, (PAIR, CHUNK)).T
+
     def one_step(step, carry):
-        block = jnp.where(step < 2, 2, jnp.where(step < 6, 1 - lax.rem(step, 2), 3))
-        pair = jnp.where((step >= 2) & (step < 6), (step - 2) // 2, lax.rem(step, 2))
-
-        for n in range(4):
-
-            @pl.when((step == 2 + n) & has_prev)
+        for n in range(pairs):
+
+            @pl.when((step == 1 + n) & has_prev)
             def _(n=n):
                 if n == 0:
                     halos[0].wait_recv()
-                halos[1 + 2 * n].wait_recv()
-                halos[2 + 2 * n].wait_recv()
-
-        for n in range(pairs):
-
-            @pl.when((step == 4 + 2 * n) & has_prev)
+                for copy in halos[1 + 4 * n : 5 + 4 * n]:
+                    copy.wait_recv()
+
+            @pl.when((step == 2 + n) & has_prev)
             def _(n=n):
                 send_prev(n)
 
-        column = pl.ds(pl.multiple_of(pair * PAIR, PAIR), PAIR)
+        outer = (step == 0) | (step == 3)
+        chains = []
+        for n in range(2):
+            block = jnp.where(step == 0, 2, jnp.where(step == 3, 3, 1 - n))
+            pair = jnp.where(outer, n, step - 1)
+            chains += [(block, pair, c) for c in range(BLOCK // CHUNK)]
         results = []
-        for c in range(BLOCK // CHUNK):
+        for block, pair, c in chains:
             start = pl.multiple_of(block * BLOCK + c * CHUNK, CHUNK)
             span = pl.ds(start, SPAN)
             mine = pl.ds(start, CHUNK)
             queries = by_head((q[pair, mine, :].astype(F32) * HS**-0.5).astype(BF16))
-            grads_in = by_head(g[pair, mine, :])
             keys = kx[pair, span, :]
             values = vx[pair, span, :]
             blocked = jnp.where(shard == 0, jnp.maximum(WINDOW - start, 0), 0)
@@ -256,29 +258,33 @@
             )
             peak = jnp.max(scores, axis=0, keepdims=True)
             raised = jnp.exp(scores - peak)
+            inverse = 1.0 / jnp.sum(raised, axis=0, keepdims=True)
+            scale = jnp.where(
+                first_head, column(inverse[:, :CHUNK]), column(inverse[:, CHUNK:])
+            )
+            grads_in = by_head((g[pair, mine, :].astype(F32) * scale).astype(BF16))
             d_attend = dot_nt(values, grads_in)
-            inverse = 1.0 / jnp.sum(raised, axis=0, keepdims=True)
             row_dot = jnp.sum(raised * d_attend, axis=0, keepdims=True) * inverse
-            attend = raised * inverse
-            d_scores = (attend * (d_attend - row_dot)).astype(BF16)
+            d_scores = (raised * (d_attend - row_dot)).astype(BF16)
             d_query = dot_nn(keys.T, d_scores) * HS**-0.5
             d_query = jnp.concatenate([d_query[:HS, :CHUNK], d_query[HS:, CHUNK:]], axis=0)
             results.append(
                 (
+                    pair,
                     span,
                     mine,
                     d_query.T.astype(BF16),
                     dot_nn(d_scores, queries),
-                    dot_nn(attend.astype(BF16), grads_in),
+                    dot_nn(raised.astype(BF16), grads_in),
                 )
             )
-        for span, mine, d_query, d_key, d_value in results:
-            grads[mine, column] = d_query
+        for pair, span, mine, d_query, d_key, d_value in results:
+            grads[mine, pl.ds(pl.multiple_of(pair * PAIR, PAIR), PAIR)] = d_query
             dk[pair, span, :] += d_key
             dv[pair, span, :] += d_value
         return carry
 
-    lax.fori_loop(0, rows // BLOCK * pairs, one_step, 0)
+    lax.fori_loop(0, rows // BLOCK, one_step, 0)
 
     for pair in range(pairs):
         grads[:, pl.ds(width + pair * PAIR, PAIR)] = dk[pair, own, :].astype(BF16)

time: 40.3 us -> 41.4 us (1.027)
  Pallas kernels: 38.3 us -> 39.2 us
    pallas_call x1, Pallas kernels: 38.3 us -> 39.2 us  [on_device(): pl.pallas_call(functools.partial(kernel, shards), out_shape=jax.ShapeDtyp...]
where the time goes in v3:
time: 41.4 us; the launch traced here: 41.1 us
  Pallas kernels  39.2 us (95%)
  local copies, waits for them, and re-layouts  1.87 us (5%)
    pallas_call x1, Pallas kernels, on_device(): pl.pallas_call(functools.partial(kernel, shards), out_shape=jax.ShapeDtyp...  39.2 us
    unnamed x1, local copies, waits for them, and re-layouts  1.87 us

profile of v3, /device:TPU:1, one launch (start us, length us, event | category | flops | bytes accessed | tf_op | source)
XLA Modules:
  0.0 41.1 jit_solution(6098453706204632656)
XLA Ops:
  0.0 39.2 %fused_backward.1 = bf16[256,1024]{1,0:T(8,128)(2,1)} custom-call(bf16[1024,256]{1,0:T(8,128)(2,1)} %q_hbm.1, bf16[1024,256]{1,0:T(8,128)(2,1)} %k_hbm.1, bf16[1024,256]{1,0:T(8,128)(2,1)} %v_hbm.1, bf16[1024,256]{1,0:T(8,128)(2,1)} %wq_hbm.1, bf16[1024,256]{1,0:T(8,128)(2,1)} %wk_hbm.1, bf16[1024,256]{1,0:T(8,128)(2,1)} %wv_hbm.1, ...), custom_call_target="tpu_custom_call" | custom-call | tf_op jit(solution)/shard_map/fused_backward/pallas_call | solution.py:397
  39.2 1.9 %copy.12 = bf16[256,1024]{1,0:T(8,128)(2,1)} copy(bf16[256,1024]{1,0:T(8,128)(2,1)} %fused_backward.1) | data formatting | bytes 1048576

commit v4 on v2

--- a/solution.py
+++ b/solution.py
@@ -15,6 +15,7 @@
 SPAN = WINDOW + CHUNK
 PAIR = 2 * HS
 PARTS = 4
+PIECES = SPAN // CHUNK
 MESH = pl.DeviceIdType.MESH
 F32 = jnp.float32
 BF16 = jnp.bfloat16
@@ -54,6 +55,10 @@
     dk,
     dv,
     grads,
+    scores,
+    d_attend,
+    p_low,
+    ds_low,
     halo_index,
     prev,
     from_next,
@@ -104,7 +109,7 @@
     loads = [
         pltpu.make_async_copy(src, dst, load_sem.at[n]) for n, (src, dst) in enumerate(moves)
     ]
-    for load in loads:
+    for load in loads[:soon]:
         load.start()
 
     barrier = pltpu.get_barrier_semaphore()
@@ -160,6 +165,8 @@
     dv[...] = jnp.zeros_like(dv)
     for load in loads[:soon]:
         load.wait()
+    for load in loads[soon:]:
+        load.start()
 
     def output_grads(block, carry):
         mine = pl.ds(pl.multiple_of(block * BLOCK, BLOCK), BLOCK)
@@ -211,7 +218,9 @@
 
     top_key = lax.broadcasted_iota(jnp.int32, (CHUNK, 2 * CHUNK), 0)
     query_pos = lax.rem(lax.broadcasted_iota(jnp.int32, (CHUNK, 2 * CHUNK), 1), CHUNK)
-    middle_key = lax.broadcasted_iota(jnp.int32, (WINDOW - CHUNK, 2 * CHUNK), 0) + CHUNK
+
+    def column(row):
+        return jnp.broadcast_to(row, (PAIR, CHUNK)).T
 
     def one_step(step, carry):
         block = jnp.where(step < 2, 2, jnp.where(step < 6, 1 - lax.rem(step, 2), 3))
@@ -232,50 +241,72 @@
             def _(n=n):
                 send_prev(n)
 
-        column = pl.ds(pl.multiple_of(pair * PAIR, PAIR), PAIR)
-        results = []
+        origin = pl.multiple_of(block * BLOCK, BLOCK)
+        window = pl.ds(origin, WINDOW + BLOCK)
+        keys_t = kx[pair, window, :].T
+        scaled_q, scaled_g = [], []
         for c in range(BLOCK // CHUNK):
-            start = pl.multiple_of(block * BLOCK + c * CHUNK, CHUNK)
-            span = pl.ds(start, SPAN)
+            start = pl.multiple_of(origin + c * CHUNK, CHUNK)
             mine = pl.ds(start, CHUNK)
-            queries = by_head((q[pair, mine, :].astype(F32) * HS**-0.5).astype(BF16))
-            grads_in = by_head(g[pair, mine, :])
-            keys = kx[pair, span, :]
-            values = vx[pair, span, :]
+            side_lanes = pl.ds(c * 2 * CHUNK, 2 * CHUNK)
             blocked = jnp.where(shard == 0, jnp.maximum(WINDOW - start, 0), 0)
-            scores = dot_nt(keys, queries)
-            scores = jnp.concatenate(
-                [
-                    jnp.where(
-                        top_key > jnp.maximum(query_pos, blocked - 1), scores[:CHUNK], -1e30
-                    ),
-                    jnp.where(middle_key >= blocked, scores[CHUNK:WINDOW], -1e30),
-                    jnp.where(top_key <= query_pos, scores[WINDOW:], -1e30),
-                ],
-                axis=0,
+            q_rows = q[pair, mine, :].astype(F32) * HS**-0.5
+            g_rows = g[pair, mine, :]
+            queries = by_head(q_rows.astype(BF16))
+            grads_in = by_head(g_rows)
+            peak = None
+            for n in range(PIECES):
+                piece = pl.ds(n * CHUNK, CHUNK)
+                part = dot_nt(kx[pair, pl.ds(start + n * CHUNK, CHUNK), :], queries)
+                if n == 0:
+                    part = jnp.where(top_key > jnp.maximum(query_pos, blocked - 1), part, -1e30)
+                elif n == PIECES - 1:
+                    part = jnp.where(top_key <= query_pos, part, -1e30)
+                else:
+                    part = jnp.where(top_key >= blocked - n * CHUNK, part, -1e30)
+                scores[c, piece, :] = part
+                best = jnp.max(part.reshape(CHUNK // 8, 8, 2 * CHUNK), axis=0)
+                peak = best if peak is None else jnp.maximum(peak, best)
+            peak = jnp.max(peak, axis=0, keepdims=True)
+            weight = jnp.zeros((8, 2 * CHUNK), F32)
+            mixed = jnp.zeros((8, 2 * CHUNK), F32)
+            for n in range(PIECES):
+                piece = pl.ds(n * CHUNK, CHUNK)
+                raised = jnp.exp(scores[c, piece, :] - peak)
+                part = dot_nt(vx[pair, pl.ds(start + n * CHUNK, CHUNK), :], grads_in)
+                d_attend[c, piece, :] = part
+                p_low[pl.ds((c + n) * CHUNK, CHUNK), side_lanes] = raised.astype(BF16)
+                weight += jnp.sum(raised.reshape(CHUNK // 8, 8, 2 * CHUNK), axis=0)
+                mixed += jnp.sum((raised * part).reshape(CHUNK // 8, 8, 2 * CHUNK), axis=0)
+            inverse = 1.0 / jnp.sum(weight, axis=0, keepdims=True)
+            row_dot = jnp.sum(mixed, axis=0, keepdims=True) * inverse
+            for n in range(PIECES):
+                piece = pl.ds(n * CHUNK, CHUNK)
+                place = pl.ds((c + n) * CHUNK, CHUNK)
+                ds_low[place, side_lanes] = (
+                    p_low[place, side_lanes].astype(F32) * (d_attend[c, piece, :] - row_dot)
+                ).astype(BF16)
+            scale = jnp.where(
+                first_head, column(inverse[:, :CHUNK]), column(inverse[:, CHUNK:])
             )
-            peak = jnp.max(scores, axis=0, keepdims=True)
-            raised = jnp.exp(scores - peak)
-            d_attend = dot_nt(values, grads_in)
-            inverse = 1.0 / jnp.sum(raised, axis=0, keepdims=True)
-            row_dot = jnp.sum(raised * d_attend, axis=0, keepdims=True) * inverse
-            attend = raised * inverse
-            d_scores = (attend * (d_attend - row_dot)).astype(BF16)
-            d_query = dot_nn(keys.T, d_scores) * HS**-0.5
+            scaled_q.append(by_head((q_rows * scale).astype(BF16)))
+            scaled_g.append(by_head((g_rows.astype(F32) * scale).astype(BF16)))
+            d_query = dot_nn(
+                keys_t[:, c * CHUNK : c * CHUNK + SPAN],
+                ds_low[pl.ds(c * CHUNK, SPAN), side_lanes],
+            ) * (inverse * HS**-0.5)
             d_query = jnp.concatenate([d_query[:HS, :CHUNK], d_query[HS:, CHUNK:]], axis=0)
-            results.append(
-                (
-                    span,
-                    mine,
-                    d_query.T.astype(BF16),
-                    dot_nn(d_scores, queries),
-                    dot_nn(attend.astype(BF16), grads_in),
-                )
+            grads[mine, pl.ds(pl.multiple_of(pair * PAIR, PAIR), PAIR)] = d_query.T.astype(BF16)
+        for held, low, rows_of in ((dk, ds_low, scaled_q), (dv, p_low, scaled_g)):
+            held[pair, pl.ds(origin, CHUNK), :] += dot_nn(
+                low[pl.ds(0, CHUNK), pl.ds(0, 2 * CHUNK)], rows_of[0]
             )
-        for span, mine, d_query, d_key, d_value in results:
-            grads[mine, column] = d_query
-            dk[pair, span, :] += d_key
-            dv[pair, span, :] += d_value
+            held[pair, pl.ds(origin + CHUNK, WINDOW), :] += dot_nn(
+                low[pl.ds(CHUNK, WINDOW), :], jnp.concatenate(rows_of, axis=0)
+            )
+            held[pair, pl.ds(origin + SPAN, CHUNK), :] += dot_nn(
+                low[pl.ds(SPAN, CHUNK), pl.ds(2 * CHUNK, 2 * CHUNK)], rows_of[1]
+            )
         return carry
 
     lax.fori_loop(0, rows // BLOCK * pairs, one_step, 0)
@@ -407,6 +438,10 @@
             vmem((pairs, rows + WINDOW, PAIR), F32),
             vmem((pairs, rows + WINDOW, PAIR), F32),
             vmem((rows, 3 * width), BF16),
+            vmem((2, SPAN, 2 * CHUNK), F32),
+            vmem((2, SPAN, 2 * CHUNK), F32),
+            vmem((SPAN + CHUNK, 4 * CHUNK), BF16),
+            vmem((SPAN + CHUNK, 4 * CHUNK), BF16),
             vmem((8, 128), jnp.int32),
             vmem((pairs, PATCH_DEV, 3 * PAIR), BF16),
             vmem((pairs, PATCH_DEV, 3 * PAIR), BF16),

time: 40.3 us -> 40.2 us (level)
  no operation moved by 1% of the time
where the time goes in v4:
time: 40.2 us; the launch traced here: 40 us
  Pallas kernels  38.1 us (95%)
  local copies, waits for them, and re-layouts  1.87 us (5%)
    pallas_call x1, Pallas kernels, on_device(): pl.pallas_call(functools.partial(kernel, shards), out_shape=jax.ShapeDtyp...  38.1 us
    unnamed x1, local copies, waits for them, and re-layouts  1.87 us

profile of v4, /device:TPU:1, one launch (start us, length us, event | category | flops | bytes accessed | tf_op | source)
XLA Modules:
  0.0 40.0 jit_solution(9015695067898722221)
XLA Ops:
  0.0 38.1 %fused_backward.1 = bf16[256,1024]{1,0:T(8,128)(2,1)} custom-call(bf16[1024,256]{1,0:T(8,128)(2,1)} %q_hbm.1, bf16[1024,256]{1,0:T(8,128)(2,1)} %k_hbm.1, bf16[1024,256]{1,0:T(8,128)(2,1)} %v_hbm.1, bf16[1024,256]{1,0:T(8,128)(2,1)} %wq_hbm.1, bf16[1024,256]{1,0:T(8,128)(2,1)} %wk_hbm.1, bf16[1024,256]{1,0:T(8,128)(2,1)} %wv_hbm.1, ...), custom_call_target="tpu_custom_call" | custom-call | tf_op jit(solution)/shard_map/fused_backward/pallas_call | solution.py:422
  38.1 1.9 %copy.12 = bf16[256,1024]{1,0:T(8,128)(2,1)} copy(bf16[256,1024]{1,0:T(8,128)(2,1)} %fused_backward.1) | data formatting | bytes 1048576

commit v5 on v4

--- a/solution.py
+++ b/solution.py
@@ -15,6 +15,7 @@
 SPAN = WINDOW + CHUNK
 PAIR = 2 * HS
 PARTS = 4
+REACH = 128
 PIECES = SPAN // CHUNK
 MESH = pl.DeviceIdType.MESH
 F32 = jnp.float32
@@ -40,7 +41,6 @@
     wout_hbm,
     dout_hbm,
     index_ref,
-    unpatch_hbm,
     out_ref,
     q,
     kx,
@@ -50,7 +50,6 @@
     wv,
     wout,
     dout,
-    unpatch,
     g,
     dk,
     dv,
@@ -105,7 +104,7 @@
             (v_hbm.at[:, lanes(pair)], vx.at[pair, own]),
         ]
     soon = len(moves)
-    moves += [(wq_hbm, wq), (wk_hbm, wk), (wv_hbm, wv), (unpatch_hbm, unpatch)]
+    moves += [(wq_hbm, wq), (wk_hbm, wk), (wv_hbm, wv)]
     loads = [
         pltpu.make_async_copy(src, dst, load_sem.at[n]) for n, (src, dst) in enumerate(moves)
     ]
@@ -209,11 +208,13 @@
             axis=1,
         )
         span = pl.ds(0, WINDOW + 128)
-        prev[pair, :, pl.ds(0, PAIR)] = dot_nn(
-            hot[:, WINDOW:], grads[pl.ds(0, 128), lanes(pair)]
+        terms = jnp.concatenate([dk[pair, span, :], dv[pair, span, :]], axis=1).astype(BF16)
+        terms = dot_nn(hot, terms).astype(BF16)
+        prev[pair, pl.ds(0, PATCH_DEV), :] = terms[:, :PAIR]
+        prev[pair, pl.ds(PATCH_DEV, PATCH_DEV), :] = terms[:, PAIR:]
+        prev[pair, pl.ds(2 * PATCH_DEV, REACH), :] = dot_nn(
+            hot[PATCH_DEV - REACH :, WINDOW:], grads[pl.ds(0, REACH), lanes(pair)]
         ).astype(BF16)
-        terms = jnp.concatenate([dk[pair, span, :], dv[pair, span, :]], axis=1).astype(BF16)
-        prev[pair, :, pl.ds(PAIR, 2 * PAIR)] = dot_nn(hot, terms).astype(BF16)
         prev_copies[pair].start()
 
     top_key = lax.broadcasted_iota(jnp.int32, (CHUNK, 2 * CHUNK), 0)
@@ -328,10 +329,13 @@
     def _():
         for pair in range(pairs):
             prev_copies[pair].wait_recv()
-            for n in range(3):
-                total[:, pl.ds(n * width + pair * PAIR, PAIR)] += from_next[
-                    pair, :, pl.ds(n * PAIR, PAIR)
+            for n in range(2):
+                total[:, pl.ds((n + 1) * width + pair * PAIR, PAIR)] += from_next[
+                    pair, pl.ds(n * PATCH_DEV, PATCH_DEV), :
                 ].astype(F32)
+            total[pl.ds(PATCH_DEV - REACH, REACH), lanes(pair)] += from_next[
+                pair, pl.ds(2 * PATCH_DEV, REACH), :
+            ].astype(F32)
 
     def project(first):
         part = total[pl.ds(first, PATCH_DEV // 2), :].astype(BF16)
@@ -375,14 +379,10 @@
         far_copies[n].wait_recv()
         done[piece, :] = (kept[piece, :] + half_in[piece, :].astype(F32)).astype(BF16)
         near_copies[n].start()
-    out_ref[pl.ds(pl.multiple_of(core * side, side), side), :] = dot_nn(
-        done[...], unpatch[...]
-    ).astype(BF16)
+    out_ref[pl.ds(pl.multiple_of(core * side, side), side), :] = done[...]
     for copy in near_copies:
         copy.wait_recv()
-    out_ref[pl.ds(pl.multiple_of((1 - core) * side, side), side), :] = dot_nn(
-        last[...], unpatch[...]
-    ).astype(BF16)
+    out_ref[pl.ds(pl.multiple_of((1 - core) * side, side), side), :] = last[...]
     for copy in core_copies + far_copies + near_copies:
         copy.wait_send()
 
@@ -395,6 +395,10 @@
     def _():
         for copy in halos:
             copy.wait_send()
+
+
+def last_product(patch_ref, unpatch_ref, out_ref):
+    out_ref[...] = dot_nn(patch_ref[...], unpatch_ref[...]).astype(BF16)
 
 
 def on_device(
@@ -419,10 +423,10 @@
     dma = pltpu.SemaphoreType.DMA
     anywhere = pl.BlockSpec(memory_space=pl.ANY)
     local = pl.BlockSpec(memory_space=pltpu.VMEM)
-    return pl.pallas_call(
+    patch_grads = pl.pallas_call(
         functools.partial(kernel, shards),
-        out_shape=jax.ShapeDtypeStruct((PATCH_DEV, out_width), BF16),
-        in_specs=[anywhere] * 8 + [local, anywhere],
+        out_shape=jax.ShapeDtypeStruct((PATCH_DEV, full), BF16),
+        in_specs=[anywhere] * 8 + [local],
         out_specs=local,
         scratch_shapes=[
             vmem((pairs, rows, PAIR), BF16),
@@ -433,7 +437,6 @@
             vmem(w_value.shape, BF16),
             vmem(w_out.shape, BF16),
             vmem(d_output.shape, BF16),
-            vmem(unpatch.shape, BF16),
             vmem((pairs, rows, PAIR), BF16),
             vmem((pairs, rows + WINDOW, PAIR), F32),
             vmem((pairs, rows + WINDOW, PAIR), F32),
@@ -443,8 +446,8 @@
             vmem((SPAN + CHUNK, 4 * CHUNK), BF16),
             vmem((SPAN + CHUNK, 4 * CHUNK), BF16),
             vmem((8, 128), jnp.int32),
-            vmem((pairs, PATCH_DEV, 3 * PAIR), BF16),
-            vmem((pairs, PATCH_DEV, 3 * PAIR), BF16),
+            vmem((pairs, 2 * PATCH_DEV + REACH, PAIR), BF16),
+            vmem((pairs, 2 * PATCH_DEV + REACH, PAIR), BF16),
             vmem((side, full), BF16),
             vmem((side, full), BF16),
             vmem((side, full), BF16),
@@ -453,7 +456,7 @@
             vmem((side, full), BF16),
             vmem((side, full), F32),
             vmem((PATCH_DEV, 3 * width), F32),
-            dma((6 + 3 * pairs,)),
+            dma((5 + 3 * pairs,)),
             dma((1 + 4 * pairs,)),
             dma((1 + 4 * pairs,)),
             dma((pairs,)),
@@ -479,8 +482,18 @@
         w_out,
         d_output,
         patch_index.reshape(8, 128),
-        unpatch,
     )
+    return pl.pallas_call(
+        last_product,
+        grid=(out_width // BLOCK,),
+        out_shape=jax.ShapeDtypeStruct((PATCH_DEV, out_width), BF16),
+        in_specs=[
+            pl.BlockSpec((PATCH_DEV, full), lambda n: (0, 0)),
+            pl.BlockSpec((full, BLOCK), lambda n: (0, n)),
+        ],
+        out_specs=pl.BlockSpec((PATCH_DEV, BLOCK), lambda n: (0, n)),
+        name="last_product",
+    )(patch_grads, unpatch)
 
 
 def solution(mesh):

time: 40.2 us -> 41.5 us (1.032)
  Pallas kernels: 38.1 us -> 41.2 us
  local copies, waits for them, and re-layouts: 1.87 us -> 0 us
    pallas_call x0 -> x1, Pallas kernels: none -> 4.22 us  [on_device(): pl.pallas_call(last_product, grid=(out_width // BLOCK,), out_shape=jax.Sh...]
    unnamed x1 -> x0, local copies, waits for them, and re-layouts: 1.87 us -> none
    pallas_call x1, Pallas kernels: 38.1 us -> 37 us  [on_device(): pl.pallas_call(functools.partial(kernel, shards), out_shape=jax.ShapeDtyp...]
where the time goes in v5:
time: 41.5 us; the launch traced here: 41.2 us
  Pallas kernels  41.2 us (99%)
    pallas_call x1, Pallas kernels, on_device(): pl.pallas_call(functools.partial(kernel, shards), out_shape=jax.ShapeDtyp...  37 us
    pallas_call x1, Pallas kernels, on_device(): pl.pallas_call(last_product, grid=(out_width // BLOCK,), out_shape=jax.Sh...  4.22 us

profile of v5, /device:TPU:1, one launch (start us, length us, event | category | flops | bytes accessed | tf_op | source)
XLA Modules:
  0.0 41.2 jit_solution(4071605999660668213)
XLA Ops:
  0.0 37.0 %fused_backward.1.patch_ref = bf16[256,1024]{1,0:T(8,128)(2,1)} custom-call(bf16[1024,256]{1,0:T(8,128)(2,1)} %q_hbm.1, bf16[1024,256]{1,0:T(8,128)(2,1)} %k_hbm.1, bf16[1024,256]{1,0:T(8,128)(2,1)} %v_hbm.1, bf16[1024,256]{1,0:T(8,128)(2,1)} %wq_hbm.1, bf16[1024,256]{1,0:T(8,128)(2,1)} %wk_hbm.1, bf16[1024,256]{1,0:T(8,128)(2,1)} %wv_hbm.1, ...), custom_call_target="tpu_custom_call" | custom-call | tf_op jit(solution)/shard_map/fused_backward/pallas_call | solution.py:426
  37.0 4.2 %last_product.1 = bf16[256,1024]{1,0:T(8,128)(2,1)} custom-call(bf16[256,1024]{1,0:T(8,128)(2,1)} %fused_backward.1.patch_ref, bf16[1024,1024]{1,0:T(8,128)(2,1)} %unpatch_ref.1), custom_call_target="tpu_custom_call" | custom-call | tf_op jit(solution)/shard_map/last_product/pallas_call | solution.py:486

commit v6 on v4

--- a/solution.py
+++ b/solution.py
@@ -15,6 +15,7 @@
 SPAN = WINDOW + CHUNK
 PAIR = 2 * HS
 PARTS = 4
+REACH = 128
 PIECES = SPAN // CHUNK
 MESH = pl.DeviceIdType.MESH
 F32 = jnp.float32
@@ -97,13 +98,22 @@
         return pl.ds(pair * PAIR, PAIR)
 
     own = pl.ds(WINDOW, rows)
-    moves = [(dout_hbm, dout), (wout_hbm, wout)]
+    tail = rows - WINDOW
+    moves = []
     for pair in range(pairs):
-        moves += [
-            (q_hbm.at[:, lanes(pair)], q.at[pair]),
-            (k_hbm.at[:, lanes(pair)], kx.at[pair, own]),
-            (v_hbm.at[:, lanes(pair)], vx.at[pair, own]),
-        ]
+        for src, dst in ((k_hbm, kx), (v_hbm, vx)):
+            moves.append((src.at[pl.ds(tail, WINDOW), lanes(pair)], dst.at[pair, pl.ds(rows, WINDOW)]))
+    first_moves = len(moves)
+    for pair in range(pairs):
+        for src, dst in ((k_hbm, kx), (v_hbm, vx)):
+            moves.append((src.at[pl.ds(0, tail), lanes(pair)], dst.at[pair, pl.ds(WINDOW, tail)]))
+    moves.append((wout_hbm, wout))
+    for pair in range(pairs):
+        moves.append((q_hbm.at[:, lanes(pair)], q.at[pair]))
+    output_moves = len(moves)
+    for n in range(rows // BLOCK):
+        mine = pl.ds(n * BLOCK, BLOCK)
+        moves.append((dout_hbm.at[mine], dout.at[mine]))
     soon = len(moves)
     moves += [(wq_hbm, wq), (wk_hbm, wk), (wv_hbm, wv), (unpatch_hbm, unpatch)]
     loads = [
@@ -137,18 +147,19 @@
             device_id_type=MESH,
         )
 
-    tail = rows - WINDOW
     halos = [halo(0, index_ref, halo_index)]
     for pair in range(pairs):
         for first in (BLOCK, 0):
-            for src, dst in ((k_hbm, kx), (v_hbm, vx)):
+            for held in (kx, vx):
                 halos.append(
                     halo(
                         len(halos),
-                        src.at[pl.ds(tail + first, BLOCK), lanes(pair)],
-                        dst.at[pair, pl.ds(first, BLOCK)],
+                        held.at[pair, pl.ds(rows + first, BLOCK)],
+                        held.at[pair, pl.ds(first, BLOCK)],
                     )
                 )
+    for load in loads[:first_moves]:
+        load.wait()
 
     @pl.when(has_next)
     def _():
@@ -163,19 +174,17 @@
 
     dk[...] = jnp.zeros_like(dk)
     dv[...] = jnp.zeros_like(dv)
-    for load in loads[:soon]:
+    for load in loads[first_moves:output_moves]:
         load.wait()
-    for load in loads[soon:]:
-        load.start()
-
-    def output_grads(block, carry):
-        mine = pl.ds(pl.multiple_of(block * BLOCK, BLOCK), BLOCK)
+
+    for n in range(rows // BLOCK):
+        loads[output_moves + n].wait()
+        mine = pl.ds(n * BLOCK, BLOCK)
         heads_grad = dot_nt(dout[mine, :], wout[...]).astype(BF16)
         for pair in range(pairs):
             g[pair, mine, :] = heads_grad[:, pair * PAIR : (pair + 1) * PAIR]
-        return carry
-
-    lax.fori_loop(0, rows // BLOCK, output_grads, 0)
+    for load in loads[soon:]:
+        load.start()
 
     def one_hot(index_row, base):
         slot = lax.broadcasted_iota(jnp.int32, (PATCH_DEV, 128), 0)
@@ -209,11 +218,13 @@
             axis=1,
         )
         span = pl.ds(0, WINDOW + 128)
-        prev[pair, :, pl.ds(0, PAIR)] = dot_nn(
-            hot[:, WINDOW:], grads[pl.ds(0, 128), lanes(pair)]
+        terms = jnp.concatenate([dk[pair, span, :], dv[pair, span, :]], axis=1).astype(BF16)
+        terms = dot_nn(hot, terms).astype(BF16)
+        prev[pair, pl.ds(0, PATCH_DEV), :] = terms[:, :PAIR]
+        prev[pair, pl.ds(PATCH_DEV, PATCH_DEV), :] = terms[:, PAIR:]
+        prev[pair, pl.ds(2 * PATCH_DEV, REACH), :] = dot_nn(
+            hot[PATCH_DEV - REACH :, WINDOW:], grads[pl.ds(0, REACH), lanes(pair)]
         ).astype(BF16)
-        terms = jnp.concatenate([dk[pair, span, :], dv[pair, span, :]], axis=1).astype(BF16)
-        prev[pair, :, pl.ds(PAIR, 2 * PAIR)] = dot_nn(hot, terms).astype(BF16)
         prev_copies[pair].start()
 
     top_key = lax.broadcasted_iota(jnp.int32, (CHUNK, 2 * CHUNK), 0)
@@ -328,10 +339,13 @@
     def _():
         for pair in range(pairs):
             prev_copies[pair].wait_recv()
-            for n in range(3):
-                total[:, pl.ds(n * width + pair * PAIR, PAIR)] += from_next[
-                    pair, :, pl.ds(n * PAIR, PAIR)
+            for n in range(2):
+                total[:, pl.ds((n + 1) * width + pair * PAIR, PAIR)] += from_next[
+                    pair, pl.ds(n * PATCH_DEV, PATCH_DEV), :
                 ].astype(F32)
+            total[pl.ds(PATCH_DEV - REACH, REACH), lanes(pair)] += from_next[
+                pair, pl.ds(2 * PATCH_DEV, REACH), :
+            ].astype(F32)
 
     def project(first):
         part = total[pl.ds(first, PATCH_DEV // 2), :].astype(BF16)
@@ -443,8 +457,8 @@
             vmem((SPAN + CHUNK, 4 * CHUNK), BF16),
             vmem((SPAN + CHUNK, 4 * CHUNK), BF16),
             vmem((8, 128), jnp.int32),
-            vmem((pairs, PATCH_DEV, 3 * PAIR), BF16),
-            vmem((pairs, PATCH_DEV, 3 * PAIR), BF16),
+            vmem((pairs, 2 * PATCH_DEV + REACH, PAIR), BF16),
+            vmem((pairs, 2 * PATCH_DEV + REACH, PAIR), BF16),
             vmem((side, full), BF16),
             vmem((side, full), BF16),
             vmem((side, full), BF16),
@@ -453,7 +467,7 @@
             vmem((side, full), BF16),
             vmem((side, full), F32),
             vmem((PATCH_DEV, 3 * width), F32),
-            dma((6 + 3 * pairs,)),
+            dma((5 + 5 * pairs + rows // BLOCK,)),
             dma((1 + 4 * pairs,)),
             dma((1 + 4 * pairs,)),
             dma((pairs,)),

time: 40.2 us -> 39.4 us (0.980)
  Pallas kernels: 38.1 us -> 37.3 us
    pallas_call x1, Pallas kernels: 38.1 us -> 37.3 us  [on_device(): pl.pallas_call(functools.partial(kernel, shards), out_shape=jax.ShapeDtyp...]
where the time goes in v6:
time: 39.4 us; the launch traced here: 39.2 us
  Pallas kernels  37.3 us (95%)
  local copies, waits for them, and re-layouts  1.87 us (5%)
    pallas_call x1, Pallas kernels, on_device(): pl.pallas_call(functools.partial(kernel, shards), out_shape=jax.ShapeDtyp...  37.3 us
    unnamed x1, local copies, waits for them, and re-layouts  1.87 us

profile of v6, /device:TPU:1, one launch (start us, length us, event | category | flops | bytes accessed | tf_op | source)
XLA Modules:
  0.0 39.2 jit_solution(17208065530650148675)
XLA Ops:
  0.0 37.3 %fused_backward.1 = bf16[256,1024]{1,0:T(8,128)(2,1)} custom-call(bf16[1024,256]{1,0:T(8,128)(2,1)} %q_hbm.1, bf16[1024,256]{1,0:T(8,128)(2,1)} %k_hbm.1, bf16[1024,256]{1,0:T(8,128)(2,1)} %v_hbm.1, bf16[1024,256]{1,0:T(8,128)(2,1)} %wq_hbm.1, bf16[1024,256]{1,0:T(8,128)(2,1)} %wk_hbm.1, bf16[1024,256]{1,0:T(8,128)(2,1)} %wv_hbm.1, ...), custom_call_target="tpu_custom_call" | custom-call | tf_op jit(solution)/shard_map/fused_backward/pallas_call | solution.py:436
  37.3 1.9 %copy.12 = bf16[256,1024]{1,0:T(8,128)(2,1)} copy(bf16[256,1024]{1,0:T(8,128)(2,1)} %fused_backward.1) | data formatting | bytes 1048576

commit v7 on v6

--- a/solution.py
+++ b/solution.py
@@ -46,9 +46,7 @@
     q,
     kx,
     vx,
-    wq,
-    wk,
-    wv,
+    weights,
     wout,
     dout,
     unpatch,
@@ -115,7 +113,11 @@
         mine = pl.ds(n * BLOCK, BLOCK)
         moves.append((dout_hbm.at[mine], dout.at[mine]))
     soon = len(moves)
-    moves += [(wq_hbm, wq), (wk_hbm, wk), (wv_hbm, wv), (unpatch_hbm, unpatch)]
+    moves += [
+        (src, weights.at[:, pl.ds(n * width, width)])
+        for n, src in enumerate((wq_hbm, wk_hbm, wv_hbm))
+    ]
+    moves.append((unpatch_hbm, unpatch))
     loads = [
         pltpu.make_async_copy(src, dst, load_sem.at[n]) for n, (src, dst) in enumerate(moves)
     ]
@@ -265,10 +267,11 @@
             g_rows = g[pair, mine, :]
             queries = by_head(q_rows.astype(BF16))
             grads_in = by_head(g_rows)
+            raw = dot_nt(kx[pair, pl.ds(start, SPAN), :], queries)
             peak = None
             for n in range(PIECES):
                 piece = pl.ds(n * CHUNK, CHUNK)
-                part = dot_nt(kx[pair, pl.ds(start + n * CHUNK, CHUNK), :], queries)
+                part = raw[n * CHUNK : (n + 1) * CHUNK, :]
                 if n == 0:
                     part = jnp.where(top_key > jnp.maximum(query_pos, blocked - 1), part, -1e30)
                 elif n == PIECES - 1:
@@ -281,10 +284,11 @@
             peak = jnp.max(peak, axis=0, keepdims=True)
             weight = jnp.zeros((8, 2 * CHUNK), F32)
             mixed = jnp.zeros((8, 2 * CHUNK), F32)
+            raw = dot_nt(vx[pair, pl.ds(start, SPAN), :], grads_in)
             for n in range(PIECES):
                 piece = pl.ds(n * CHUNK, CHUNK)
                 raised = jnp.exp(scores[c, piece, :] - peak)
-                part = dot_nt(vx[pair, pl.ds(start + n * CHUNK, CHUNK), :], grads_in)
+                part = raw[n * CHUNK : (n + 1) * CHUNK, :]
                 d_attend[c, piece, :] = part
                 p_low[pl.ds((c + n) * CHUNK, CHUNK), side_lanes] = raised.astype(BF16)
                 weight += jnp.sum(raised.reshape(CHUNK // 8, 8, 2 * CHUNK), axis=0)
@@ -349,11 +353,7 @@
 
     def project(first):
         part = total[pl.ds(first, PATCH_DEV // 2), :].astype(BF16)
-        return (
-            dot_nt(part[:, :width], wq[...])
-            + dot_nt(part[:, width : 2 * width], wk[...])
-            + dot_nt(part[:, 2 * width :], wv[...])
-        )
+        return dot_nt(part, weights[...])
 
     side = PATCH_DEV // 2
     part = side // PARTS
@@ -442,9 +442,7 @@
             vmem((pairs, rows, PAIR), BF16),
             vmem((pairs, rows + WINDOW, PAIR), BF16),
             vmem((pairs, rows + WINDOW, PAIR), BF16),
-            vmem(w_query.shape, BF16),
-            vmem(w_key.shape, BF16),
-            vmem(w_value.shape, BF16),
+            vmem((full, 3 * width), BF16),
             vmem(w_out.shape, BF16),
             vmem(d_output.shape, BF16),
             vmem(unpatch.shape, BF16),

time: 39.4 us -> 39.3 us (level)
  no operation moved by 1% of the time
where the time goes in v7:
time: 39.3 us; the launch traced here: 39.1 us
  Pallas kernels  37.2 us (95%)
  local copies, waits for them, and re-layouts  1.87 us (5%)
    pallas_call x1, Pallas kernels, on_device(): pl.pallas_call(functools.partial(kernel, shards), out_shape=jax.ShapeDtyp...  37.2 us
    unnamed x1, local copies, waits for them, and re-layouts  1.87 us

profile of v7, /device:TPU:1, one launch (start us, length us, event | category | flops | bytes accessed | tf_op | source)
XLA Modules:
  0.0 39.1 jit_solution(11279091712902792532)
XLA Ops:
  0.0 37.2 %fused_backward.1 = bf16[256,1024]{1,0:T(8,128)(2,1)} custom-call(bf16[1024,256]{1,0:T(8,128)(2,1)} %q_hbm.1, bf16[1024,256]{1,0:T(8,128)(2,1)} %k_hbm.1, bf16[1024,256]{1,0:T(8,128)(2,1)} %v_hbm.1, bf16[1024,256]{1,0:T(8,128)(2,1)} %wq_hbm.1, bf16[1024,256]{1,0:T(8,128)(2,1)} %wk_hbm.1, bf16[1024,256]{1,0:T(8,128)(2,1)} %wv_hbm.1, ...), custom_call_target="tpu_custom_call" | custom-call | tf_op jit(solution)/shard_map/fused_backward/pallas_call | solution.py:436
  37.2 1.9 %copy.12 = bf16[256,1024]{1,0:T(8,128)(2,1)} copy(bf16[256,1024]{1,0:T(8,128)(2,1)} %fused_backward.1) | data formatting | bytes 1048576

commit v8 on v7

--- a/solution.py
+++ b/solution.py
@@ -165,7 +165,7 @@
 
     @pl.when(has_next)
     def _():
-        for copy in halos:
+        for copy in halos[:5]:
             copy.start()
 
     @pl.when(shard == 0)
@@ -238,6 +238,11 @@
     def one_step(step, carry):
         block = jnp.where(step < 2, 2, jnp.where(step < 6, 1 - lax.rem(step, 2), 3))
         pair = jnp.where((step >= 2) & (step < 6), (step - 2) // 2, lax.rem(step, 2))
+
+        @pl.when((step == 2) & has_next)
+        def _():
+            for copy in halos[5:]:
+                copy.start()
 
         for n in range(4):
 

time: 39.3 us -> 38.1 us (0.969)
  Pallas kernels: 37.2 us -> 35.9 us
    pallas_call x1, Pallas kernels: 37.2 us -> 35.9 us  [on_device(): pl.pallas_call(functools.partial(kernel, shards), out_shape=jax.ShapeDtyp...]
where the time goes in v8:
time: 38.1 us; the launch traced here: 37.8 us
  Pallas kernels  35.9 us (94%)
  local copies, waits for them, and re-layouts  1.87 us (5%)
    pallas_call x1, Pallas kernels, on_device(): pl.pallas_call(functools.partial(kernel, shards), out_shape=jax.ShapeDtyp...  35.9 us
    unnamed x1, local copies, waits for them, and re-layouts  1.87 us

profile of v8, /device:TPU:1, one launch (start us, length us, event | category | flops | bytes accessed | tf_op | source)
XLA Modules:
  0.0 37.8 jit_solution(743984230271975075)
XLA Ops:
  0.0 35.9 %fused_backward.1 = bf16[256,1024]{1,0:T(8,128)(2,1)} custom-call(bf16[1024,256]{1,0:T(8,128)(2,1)} %q_hbm.1, bf16[1024,256]{1,0:T(8,128)(2,1)} %k_hbm.1, bf16[1024,256]{1,0:T(8,128)(2,1)} %v_hbm.1, bf16[1024,256]{1,0:T(8,128)(2,1)} %wq_hbm.1, bf16[1024,256]{1,0:T(8,128)(2,1)} %wk_hbm.1, bf16[1024,256]{1,0:T(8,128)(2,1)} %wv_hbm.1, ...), custom_call_target="tpu_custom_call" | custom-call | tf_op jit(solution)/shard_map/fused_backward/pallas_call | solution.py:441
  35.9 1.9 %copy.12 = bf16[256,1024]{1,0:T(8,128)(2,1)} copy(bf16[256,1024]{1,0:T(8,128)(2,1)} %fused_backward.1) | data formatting | bytes 1048576
